TPU v7x, 128 devices: a whole 4x4x4 slice. The times are simulated.
128 devices in a mesh: face: 4 (over z), tile: 32 (over y, x, core).
Axes of the slice: x: 4, y: 4, z: 4, core: 2. Of those that a mesh axis runs over, the one named last changes fastest.
Arguments:
- profiles: bfloat16 [131072, 2048], P(('face', 'tile'))
- sun_cos: bfloat16 [131072], P(('face', 'tile')), may hold values from 0.049804688 to 1
- albedo: bfloat16 [131072], P(('face', 'tile')), may hold values from 0.049804688 to 0.796875
- span_order: int32 [128, 1024], P(('face', 'tile')), may hold values from 0 to 1023, as said below
- keep_list: int32 [128, 384], P(('face', 'tile')), may hold values from 0 to 1023, as said below
- ship_list: int32 [128, 128], P(('face', 'tile')), may hold values from 0 to 1023, as said below
- ship_count: int32 [128], P(('face', 'tile')), may hold values from 0 to 128, as said below
- w_hidden: bfloat16 [32, 128], replicated, may hold values from -1 to 1
- optical_weight: bfloat16 [128, 336], replicated, may hold values from -0.5 to 0.5
- solar_weight: float32 [112], replicated, may hold values from 0.005 to 0.05
Outputs:
- heating: float32 [64, 131072], P(None, ('face', 'tile'))
- surface_down: float32 [131072], P(('face', 'tile'))
Inputs may be any that keep to these rules, and one draw needn't show every extreme that they name: `span_order`: each row is a permutation of the device's 1024 local column slots. `keep_list`: row e names distinct span slots of device e, none of them in row e of ship_list. `ship_list`: row e names distinct span slots of device e, none of them in row e of keep_list. `ship_count`: some device has exactly 128.
All inputs are finite; a program needn't handle non-finite values.
Results may differ from a plain program's by a relative error of at most 0.00052.
Values may be sent and summed in bfloat16 or wider, within the bound.
A program may use at most 192 MiB of HBM per device.

v0:
```python
import jax
import jax.numpy as jnp
from jax import lax
from jax.sharding import PartitionSpec as P


def passed_along(shard, axis, by):
    devices = lax.axis_size(axis)
    return lax.ppermute(shard, axis, [(i, (i + by) % devices) for i in range(devices)])


def two_stream(optical_properties, layer_mass, cosine, surface_albedo, solar_weight):
    levels = layer_mass.shape[0]
    gpoints = solar_weight.shape[0]
    depth = 2.0 * layer_mass[:, None, :] * jnp.exp(optical_properties[:, :gpoints, :]) / levels
    single_albedo = 0.98 * jax.nn.sigmoid(optical_properties[:, gpoints : 2 * gpoints, :])
    backscatter = 0.5 * (1.0 - 0.8 * jnp.tanh(optical_properties[:, 2 * gpoints :, :]))
    direct_beam = jnp.exp(-depth / cosine[None, None, :])
    reflect = single_albedo * backscatter * (1.0 - direct_beam)
    transmit = direct_beam + single_albedo * (1.0 - backscatter) * (1.0 - direct_beam)

    def upward(reflectance_lower, layer_pair):
        reflect_here, transmit_here = layer_pair
        denominator = 1.0 - reflect_here * reflectance_lower
        reflectance_upper = (
            reflect_here + transmit_here * transmit_here * reflectance_lower / denominator
        )
        return (reflectance_upper, (reflectance_upper, transmit_here / denominator))

    ground = jnp.broadcast_to(surface_albedo[None, :], (gpoints, cosine.shape[0]))
    top_reflect, stacks = lax.scan(upward, ground, (reflect, transmit), reverse=True)

    def downward(flux_down, layer_pair):
        reflect_here, factor_here = layer_pair
        net_flux = jnp.sum(flux_down * (1.0 - reflect_here), axis=0)
        return (flux_down * factor_here, net_flux)

    incident = solar_weight[:, None] * cosine[None, :]
    bottom_flux, net_levels = lax.scan(downward, incident, stacks)
    net_ground = jnp.sum(bottom_flux * (1.0 - surface_albedo[None, :]), axis=0)
    net_all = jnp.concatenate([net_levels, net_ground[None, :]], axis=0)
    heating_rates = levels * (net_all[:-1] - net_all[1:]) / layer_mass
    return (heating_rates, jnp.sum(bottom_flux, axis=0))


def optics_block(profile_rows, cosine_rows, albedo_rows, w_hidden, optical_weight, solar_weight):
    feature_count = w_hidden.shape[0]
    features = profile_rows.reshape(profile_rows.shape[0], -1, feature_count)
    preact = jnp.einsum("clf,fh->lch", features, w_hidden, preferred_element_type=jnp.float32)
    hidden_activations = jax.nn.silu(preact).astype(jnp.bfloat16)
    optical_properties = jnp.einsum(
        "lch,hp->lpc", hidden_activations, optical_weight, preferred_element_type=jnp.float32
    )
    layer_mass = features[:, :, 0].astype(jnp.float32).T
    return two_stream(
        optical_properties,
        layer_mass,
        cosine_rows.astype(jnp.float32),
        albedo_rows.astype(jnp.float32),
        solar_weight,
    )


def radiate(profile_rows, cosine_rows, albedo_rows, w_hidden, optical_weight, solar_weight):
    row_count = profile_rows.shape[0]
    block_size = 512
    blocks = row_count // block_size
    packed = (
        profile_rows.reshape(blocks, block_size, -1),
        cosine_rows.reshape(blocks, block_size),
        albedo_rows.reshape(blocks, block_size),
    )

    def one_block(block_data):
        return optics_block(
            block_data[0], block_data[1], block_data[2], w_hidden, optical_weight, solar_weight
        )

    heating_rates, surface_flux = lax.map(one_block, packed)
    level_count = heating_rates.shape[1]
    return (
        jnp.moveaxis(heating_rates, 0, 1).reshape(level_count, row_count),
        surface_flux.reshape(row_count),
    )


def on_device(
    profiles,
    sun_cos,
    albedo,
    span_order,
    keep_list,
    ship_list,
    ship_count,
    w_hidden,
    optical_weight,
    solar_weight,
):
    columns = profiles.shape[0]
    devices = lax.axis_size(("face", "tile"))
    tile_count = lax.axis_size("tile")
    per_peer = columns // devices
    slot_permutation = span_order[0]
    send_profile = profiles[slot_permutation].reshape(devices, per_peer, -1)
    send_cosine = sun_cos[slot_permutation].reshape(devices, per_peer)
    send_albedo = albedo[slot_permutation].reshape(devices, per_peer)
    got_profile, got_cosine, got_albedo = (
        lax.all_to_all(send_profile, ("face", "tile"), split_axis=0, concat_axis=0, tiled=True),
        lax.all_to_all(send_cosine, ("face", "tile"), split_axis=0, concat_axis=0, tiled=True),
        lax.all_to_all(send_albedo, ("face", "tile"), split_axis=0, concat_axis=0, tiled=True),
    )
    span_profile = got_profile.reshape(columns, -1)
    span_cosine = got_cosine.reshape(columns)
    span_albedo = got_albedo.reshape(columns)
    keep_slots = keep_list[0]
    ship_slots = ship_list[0]
    ship_live = jnp.arange(ship_slots.shape[0]) < ship_count[0]
    half_tile = tile_count // 2
    help_profile, help_cosine, help_albedo = passed_along(
        (span_profile[ship_slots], span_cosine[ship_slots], span_albedo[ship_slots]),
        "tile",
        half_tile,
    )
    kept_profile = span_profile[keep_slots]
    kept_cosine = span_cosine[keep_slots]
    kept_albedo = span_albedo[keep_slots]
    keep_rows = keep_slots.shape[0]
    joined_heat, joined_surface = radiate(
        jnp.concatenate([kept_profile, help_profile], axis=0),
        jnp.concatenate([kept_cosine, help_cosine], axis=0),
        jnp.concatenate([kept_albedo, help_albedo], axis=0),
        w_hidden,
        optical_weight,
        solar_weight,
    )
    kept_heat = joined_heat[:, :keep_rows]
    retained_surface_flux = joined_surface[:keep_rows]
    help_heat = joined_heat[:, keep_rows:]
    help_surface = joined_surface[keep_rows:]
    back_heat, back_surface = passed_along((help_heat, help_surface), "tile", half_tile)
    back_heat = jnp.where(ship_live[None, :], back_heat, 0.0)
    back_surface = jnp.where(ship_live, back_surface, 0.0)
    level_count = back_heat.shape[0]
    span_heat = (
        jnp.zeros((level_count, columns), jnp.float32)
        .at[:, keep_slots]
        .set(kept_heat)
        .at[:, ship_slots]
        .set(back_heat)
    )
    span_surface = (
        jnp.zeros((columns,), jnp.float32)
        .at[keep_slots]
        .set(retained_surface_flux)
        .at[ship_slots]
        .set(back_surface)
    )
    home_heat, home_surface = (
        lax.all_to_all(
            span_heat.reshape(level_count, devices, per_peer),
            ("face", "tile"),
            split_axis=1,
            concat_axis=1,
            tiled=True,
        ),
        lax.all_to_all(
            span_surface.reshape(1, devices, per_peer),
            ("face", "tile"),
            split_axis=1,
            concat_axis=1,
            tiled=True,
        ),
    )
    heating = (
        jnp.zeros_like(span_heat)
        .at[:, slot_permutation]
        .set(home_heat.reshape(level_count, columns))
    )
    surface_down = (
        jnp.zeros_like(span_surface).at[slot_permutation].set(home_surface.reshape(columns))
    )
    return (heating, surface_down)


def solution(mesh):
    placed = (
        P(("face", "tile"), None),
        P(("face", "tile")),
        P(("face", "tile")),
        P(("face", "tile"), None),
        P(("face", "tile"), None),
        P(("face", "tile"), None),
        P(("face", "tile")),
        P(),
        P(),
        P(),
    )
    return jax.shard_map(
        on_device,
        mesh=mesh,
        in_specs=placed,
        out_specs=(P(None, ("face", "tile")), P(("face", "tile"))),
        check_vma=False,
    )
```

profile of v0, /device:TPU:1, one launch (start us, length us, event | category | flops | bytes accessed | tf_op | source)
XLA Modules:
  0.0 450.0 jit_solution(11024499790839569106)
XLA Ops:
  1.4 6.3 %gather_fusion = bf16[1024]{0:T(1024)(128)(2,1)S(1)} fusion(bf16[1024]{0:T(1024)(128)(2,1)} %param.15, s32[1024]{0:T(1024)S(1)} %broadcast_clamp_fusion), kind=kCustom, calls=%fused_computation | custom fusion | bytes 8192 | tf_op jit(solution)/shard_map/gather | solution.py:105
  8.5 11.5 %all-to-all-start = ((bf16[128,1,8]{2,1,0:T(2,128)(2,1)}), bf16[128,1,8]{2,1,0:T(2,128)(2,1)S(1)}, u32[]{:S(2)}, u32[]{:S(2)}) async-start(bf16[128,1,8]{2,1,0:T(2,128)(2,1)} %all_to_all.28), calls=%async_computation | async-start | bytes 131072 | tf_op jit(solution)/shard_map/all_to_all | solution.py:109
  20.0 6.3 %gather_fusion.3 = bf16[1024]{0:T(1024)(128)(2,1)S(1)} fusion(bf16[1024]{0:T(1024)(128)(2,1)} %param.16, s32[1024]{0:T(1024)S(1)} %broadcast_clamp_fusion), kind=kCustom, calls=%fused_computation.3 | custom fusion | bytes 8192 | tf_op jit(solution)/shard_map/gather | solution.py:106
  27.1 2.4 all-to-all-done
  29.5 7.3 %all-to-all-start.1 = ((bf16[128,1,8]{2,1,0:T(2,128)(2,1)}), bf16[128,1,8]{2,1,0:T(2,128)(2,1)S(1)}, u32[]{:S(2)}, u32[]{:S(2)}) async-start(bf16[128,1,8]{2,1,0:T(2,128)(2,1)} %all_to_all.29), calls=%async_computation.1 | async-start | bytes 131072 | tf_op jit(solution)/shard_map/all_to_all | solution.py:110
  36.8 11.6 %gather_fusion.6 = bf16[1024,2048]{1,0:T(8,128)(2,1)} fusion(bf16[1024,2048]{1,0:T(8,128)(2,1)} %param.14, s32[1024]{0:T(1024)S(1)} %broadcast_clamp_fusion), kind=kCustom, calls=%fused_computation.6 | custom fusion | bytes 8392704 | tf_op jit(solution)/shard_map/gather | solution.py:104
  48.4 10.2 %all-to-all-start.2 = ((bf16[128,8,2048]{2,1,0:T(8,128)(2,1)}), bf16[128,8,2048]{2,1,0:T(8,128)(2,1)}, u32[]{:S(2)}, u32[]{:S(2)}) async-start(bf16[128,8,2048]{2,1,0:T(8,128)(2,1)} %bitcast.106), calls=%async_computation.2 | async-start | bytes 8388608 | tf_op jit(solution)/shard_map/all_to_all | solution.py:108
  61.0 2.8 gather_fusion.1
  65.3 2.8 gather_fusion.4
  68.2 3.0 collective-permute-start.1
  71.2 40.1 %all-to-all-done.2 = bf16[128,8,2048]{2,1,0:T(8,128)(2,1)} async-done(((bf16[128,8,2048]{2,1,0:T(8,128)(2,1)}), bf16[128,8,2048]{2,1,0:T(8,128)(2,1)}, u32[]{:S(2)}, u32[]{:S(2)}) %all-to-all-start.2) | async-done | bytes 4194336 | tf_op jit(solution)/shard_map/all_to_all | solution.py:108
  111.3 4.2 gather_fusion.8
  116.0 7.8 %gather_fusion.7 = bf16[384,2048]{1,0:T(8,128)(2,1)} fusion(bf16[1024,2048]{1,0:T(8,128)(2,1)} %bitcast.13, s32[1024]{0:T(1024)S(1)} %pad_clamp_fusion.1), kind=kCustom, calls=%fused_computation.7 | custom fusion | bytes 3147264 | tf_op jit(solution)/shard_map/gather | solution.py:124
  123.8 5.9 %collective-permute-done.2 = bf16[128,2048]{1,0:T(8,128)(2,1)S(1)} collective-permute-done((bf16[128,2048]{1,0:T(8,128)(2,1)S(1)}, bf16[128,2048]{1,0:T(8,128)(2,1)S(1)}, u32[]{:S(2)}, u32[]{:S(2)}) %collective-permute-start.2) | collective-permute-done | bytes 524320 | tf_op jit(solution)/shard_map/ppermute | solution.py:9
  131.4 2.5 copy.22
  135.0 20.7 %convolution_bitcast_fusion = f32[64,336,512]{2,1,0:T(8,128)} fusion(bf16[512,64,32]{0,2,1:T(8,128)(2,1)} %bitcast.108, bf16[128,336]{0,1:T(8,128)(2,1)S(1)} %copy-done, bf16[32,128]{1,0:T(8,128)(2,1)S(1)} %copy-done.4), kind=kOutput, calls=%fused_computation.27 | convolution fusion | flops 3107979264 | bytes 46231552 | tf_op jit(solution)/shard_map/while/body/eval_jaxpr/lch,hp->lpc/dot_general | solution.py:51
  155.7 26.2 %multiply_add_fusion = (f32[64,112,512]{2,1,0:T(8,128)}, f32[64,112,512]{2,1,0:T(8,128)}) fusion(f32[64,336,512]{2,1,0:T(8,128)} %convolution_bitcast_fusion, f32[512]{0:T(512)S(1)} %maximum_convert_fusion, f32[64,512]{1,0:T(8,128)S(1)} %bitcast_multiply_fusion.5), kind=kLoop, calls=%fused_computation.49 | loop fusion | flops 66060288 | bytes 73533440 | tf_op jit(solution)/shard_map/while/body/eval_jaxpr/add | solution.py:20
  181.9 7.1 %broadcast.144 = f32[64,112,512]{2,1,0:T(8,128)} broadcast(f32[]{:T(128)} %constant.107.clone.1), dimensions={} | broadcast | bytes 14680068 | tf_op jit(solution)/shard_map/broadcast.2
  189.0 7.1 %broadcast.144.clone = f32[64,112,512]{2,1,0:T(8,128)} broadcast(f32[]{:T(128)} %constant.107.clone.1), dimensions={} | broadcast | bytes 14680068 | tf_op jit(solution)/shard_map/broadcast.2
  196.1 127.4 %while.43 = (s32[]{:T(128)}, f32[112,512]{1,0:T(8,128)S(1)}, f32[64,112,512]{2,1,0:T(8,128)}, f32[64,112,512]{2,1,0:T(8,128)}, f32[64,112,512]{2,1,0:T(8,128)}, ...) while((s32[]{:T(128)}, f32[112,512]{1,0:T(8,128)S(1)}, f32[64,112,512]{2,1,0:T(8,128)}, ...), condition=%wide.region_1.2_spmd, body=%wide.region_0.1_spmd.sunk | while | flops 401411 | bytes 1376357 | solution.py:31
  225.8 2.0 bitcast_dynamic-update-slice_fusion.3
  243.8 2.0 bitcast_dynamic-update-slice_fusion.3
  249.8 2.0 bitcast_dynamic-update-slice_fusion.3
  323.4 79.7 %while.44 = (s32[]{:T(128)}, f32[112,512]{1,0:T(8,128)S(1)}, f32[64,512]{1,0:T(8,128)S(1)}, f32[64,112,512]{2,1,0:T(8,128)}, f32[64,112,512]{2,1,0:T(8,128)}, /*index=5*/s32[]{:T(128)}, s32[]{:T(128)}) while((s32[]{:T(128)}, f32[112,512]{1,0:T(8,128)S(1)}, f32[64,512]{1,0:T(8,128)S(1)}, f32[64,112,512]{2,1,0:T(8,128)}, ...), condition=%wide.region_4.5_spmd, body=%wide.region_2.4_spmd.sunk | while | flops 228866 | bytes 923733 | solution.py:39
  404.1 2.5 collective-permute-start.3
  406.6 2.9 scatter_custom_fusion.3
  412.8 5.8 %all-to-all-start.4 = ((f32[1,128,8]{2,0,1:T(1,128)}), f32[1,128,8]{2,0,1:T(1,128)S(1)}, u32[]{:S(2)}, u32[]{:S(2)}) async-start(f32[1,128,8]{2,0,1:T(1,128)} %bitcast.27), calls=%async_computation.4 | async-start | bytes 131072 | tf_op jit(solution)/shard_map/all_to_all | solution.py:166
  420.9 7.4 %all-to-all-done.4 = f32[1,128,8]{2,0,1:T(1,128)S(1)} async-done(((f32[1,128,8]{2,0,1:T(1,128)}), f32[1,128,8]{2,0,1:T(1,128)S(1)}, u32[]{:S(2)}, u32[]{:S(2)}) %all-to-all-start.4) | async-done | bytes 4128 | tf_op jit(solution)/shard_map/all_to_all | solution.py:166
  428.3 4.5 all-to-all-start.3
  434.2 4.9 %scatter_custom_fusion.5 = f32[1024]{0:T(1024)} fusion(s32[1024]{0:T(1024)S(1)} %bitcast.111, f32[1024]{0:T(1024)S(1)} %reshape.310, f32[]{:T(128)} %constant.107.clone.1), kind=kCustom, calls=%fused_computation.75 | custom fusion | bytes 4100 | tf_op jit(solution)/shard_map/scatter | solution.py:180
  439.1 4.8 %all-to-all-done.3 = f32[128,1,512]{2,1,0:T(1,128)S(1)} async-done(((f32[128,1,512]{2,1,0:T(1,128)}), f32[128,1,512]{2,1,0:T(1,128)S(1)}, u32[]{:S(2)}, u32[]{:S(2)}) %all-to-all-start.3) | async-done | bytes 262176 | tf_op jit(solution)/shard_map/all_to_all | solution.py:159
  445.8 3.3 scatter_custom_fusion.2
  (255 shorter events, 218.9 us)
Async XLA Ops:
  0.6 134.4 %copy-start = (bf16[128,336]{0,1:T(8,128)(2,1)S(1)}, bf16[128,336]{0,1:T(8,128)(2,1)}, u32[]{:S(2)}) copy-start(bf16[128,336]{0,1:T(8,128)(2,1)} %param.22) | copy-start | bytes 258052
  8.5 21.0 %all-to-all-start = ((bf16[128,1,8]{2,1,0:T(2,128)(2,1)}), bf16[128,1,8]{2,1,0:T(2,128)(2,1)S(1)}, u32[]{:S(2)}, u32[]{:S(2)}) async-start(bf16[128,1,8]{2,1,0:T(2,128)(2,1)} %all_to_all.28), calls=%async_computation | async-start | bytes 131072 | tf_op jit(solution)/shard_map/all_to_all | solution.py:109
  29.5 18.9 %all-to-all-start.1 = ((bf16[128,1,8]{2,1,0:T(2,128)(2,1)}), bf16[128,1,8]{2,1,0:T(2,128)(2,1)S(1)}, u32[]{:S(2)}, u32[]{:S(2)}) async-start(bf16[128,1,8]{2,1,0:T(2,128)(2,1)} %all_to_all.29), calls=%async_computation.1 | async-start | bytes 131072 | tf_op jit(solution)/shard_map/all_to_all | solution.py:110
  36.8 22.5 %copy-start.2 = (s32[1,384]{1,0:T(1,128)S(1)}, s32[1,384]{1,0:T(1,128)}, u32[]{:S(2)}) copy-start(s32[1,384]{1,0:T(1,128)} %param.18) | copy-start | bytes 4612
  36.8 22.5 %copy-start.5 = (s32[1,128]{1,0:T(1,128)S(1)}, s32[1,128]{1,0:T(1,128)}, u32[]{:S(2)}) copy-start(s32[1,128]{1,0:T(1,128)} %param.19) | copy-start | bytes 1540
  48.4 67.5 %copy-start.3 = (f32[112]{0:T(128)S(1)}, f32[112]{0:T(128)}, u32[]{:S(2)}) copy-start(f32[112]{0:T(128)} %param.23) | copy-start | bytes 1348
  48.4 62.9 %all-to-all-start.2 = ((bf16[128,8,2048]{2,1,0:T(8,128)(2,1)}), bf16[128,8,2048]{2,1,0:T(8,128)(2,1)}, u32[]{:S(2)}, u32[]{:S(2)}) async-start(bf16[128,8,2048]{2,1,0:T(8,128)(2,1)} %bitcast.106), calls=%async_computation.2 | async-start | bytes 8388608 | tf_op jit(solution)/shard_map/all_to_all | solution.py:108
  64.1 70.9 %copy-start.4 = (bf16[32,128]{1,0:T(8,128)(2,1)S(1)}, bf16[32,128]{1,0:T(8,128)(2,1)}, u32[]{:S(2)}) copy-start(bf16[32,128]{1,0:T(8,128)(2,1)} %param.21) | copy-start | bytes 24580
  68.2 47.7 %collective-permute-start.1 = (bf16[128]{0:T(256)(128)(2,1)S(1)}, bf16[128]{0:T(256)(128)(2,1)S(1)}, u32[]{:S(2)}, u32[]{:S(2)}) collective-permute-start(bf16[128]{0:T(256)(128)(2,1)S(1)} %gather_fusion.5), channel_id=1, source_target_pairs={{0,16},{1,17},{2,18},{3,19},{4,20},{5,21},{6,22},{7,23},{8,24},{9,... | collective-permute-start | bytes 776 | tf_op jit(solution)/shard_map/ppermute | solution.py:9
  71.1 44.7 %collective-permute-start = (bf16[128]{0:T(256)(128)(2,1)S(1)}, bf16[128]{0:T(256)(128)(2,1)S(1)}, u32[]{:S(2)}, u32[]{:S(2)}) collective-permute-start(bf16[128]{0:T(256)(128)(2,1)S(1)} %gather_fusion.2), channel_id=1, source_target_pairs={{0,16},{1,17},{2,18},{3,19},{4,20},{5,21},{6,22},{7,23},{8,24},{9,... | collective-permute-start | bytes 776 | tf_op jit(solution)/shard_map/ppermute | solution.py:9
  115.5 14.3 %collective-permute-start.2 = (bf16[128,2048]{1,0:T(8,128)(2,1)S(1)}, bf16[128,2048]{1,0:T(8,128)(2,1)S(1)}, u32[]{:S(2)}, u32[]{:S(2)}) collective-permute-start(bf16[128,2048]{1,0:T(8,128)(2,1)S(1)} %gather_fusion.8), channel_id=1, source_target_pairs={{0,16},{1,17},{2,18},{3,19},{4,20},{5,21},{6,22},{7,23},{8,24},{9,... | collective-permute-start | bytes 1572872 | tf_op jit(solution)/shard_map/ppermute | solution.py:9
  181.9 268.1 %copy-start.1 = (bf16[128,336]{0,1:T(8,128)(2,1)S(1)}, bf16[128,336]{0,1:T(8,128)(2,1)}, u32[]{:S(2)}) copy-start(bf16[128,336]{0,1:T(8,128)(2,1)} %param.22) | copy-start | bytes 258052
  403.2 7.8 %collective-permute-start.4 = (f32[128]{0:T(128)S(1)}, f32[128]{0:T(128)S(1)}, u32[]{:S(2)}, u32[]{:S(2)}) collective-permute-start(f32[128]{0:T(128)S(1)} %slice.41), channel_id=1, source_target_pairs={{0,16},{1,17},{2,18},{3,19},{4,20},{5,21},{6,22},{7,23},{8,24},{9,... | collective-permute-start | bytes 1544 | tf_op jit(solution)/shard_map/ppermute | solution.py:9
  404.1 14.5 %collective-permute-start.3 = (f32[64,128]{1,0:T(8,128)S(1)}, f32[64,128]{1,0:T(8,128)S(1)}, u32[]{:S(2)}, u32[]{:S(2)}) collective-permute-start(f32[64,128]{1,0:T(8,128)S(1)} %slice.65), channel_id=1, source_target_pairs={{0,16},{1,17},{2,18},{3,19},{4,20},{5,21},{6,22},{7,23},{8,24},{9,... | collective-permute-start | bytes 98312 | tf_op jit(solution)/shard_map/ppermute | solution.py:9
  412.8 15.6 %all-to-all-start.4 = ((f32[1,128,8]{2,0,1:T(1,128)}), f32[1,128,8]{2,0,1:T(1,128)S(1)}, u32[]{:S(2)}, u32[]{:S(2)}) async-start(f32[1,128,8]{2,0,1:T(1,128)} %bitcast.27), calls=%async_computation.4 | async-start | bytes 131072 | tf_op jit(solution)/shard_map/all_to_all | solution.py:166
  428.3 15.6 %all-to-all-start.3 = ((f32[128,1,512]{2,1,0:T(1,128)}), f32[128,1,512]{2,1,0:T(1,128)S(1)}, u32[]{:S(2)}, u32[]{:S(2)}) async-start(f32[128,1,512]{2,1,0:T(1,128)} %reshape.336), calls=%async_computation.3 | async-start | bytes 524288 | tf_op jit(solution)/shard_map/all_to_all | solution.py:159
where the time goes:
time: 453 us; the launch traced here: 450 us
  other arithmetic  234 us (52%)
  local copies, waits for them, and re-layouts  85.3 us (19%)
  waiting for transfers between devices  60.7 us (13%)
  starting transfers between devices  45.9 us (10%)
  matrix products  20.7 us (5%)
    dynamic_update_slice x64, other arithmetic, two_stream(): lax.scan(upward, ground, (reflect, transmit), reverse=True)  127 us
    reduce_sum x64, other arithmetic, downward(): net_flux = jnp.sum(flux_down * (1.0 - reflect_here), axis=0)  74.6 us
    all_to_all x1, waiting for transfers between devices, on_device(): lax.all_to_all(send_profile, ('face', 'tile'), split_axis=0, concat_axis=...  40.1 us
    add x1, other arithmetic, two_stream(): direct_beam + single_albedo * (1.0 - backscatter) * (1.0 - direct_beam)  26.2 us
    dot_general x1, matrix products, optics_block(): jnp.einsum('lch,hp->lpc', hidden_activations, optical_weight, preferred_e...  20.7 us
    another operation x2, local copies, waits for them, and re-layouts  14.2 us
    gather x1, local copies, waits for them, and re-layouts, on_device(): send_profile = profiles[slot_permutation].reshape(devices, per_peer, -1)  11.6 us
    all_to_all x1, starting transfers between devices, on_device(): lax.all_to_all(send_cosine, ('face', 'tile'), split_axis=0, concat_axis=0...  11.5 us
  transfers between devices with their start and end apart: 10, of which 5 were waited for; matrix products, arithmetic and copies ran while one was open for 12% of the time, Pallas kernels for 0%

commit v1 on v0

v1 whole, which is shorter than its diff:
```python
import functools, math
import jax, jax.numpy as jnp
from jax import lax
from jax.experimental import pallas as pl
from jax.experimental.pallas import tpu as pltpu
from jax.sharding import PartitionSpec as P

L, F, H, G = 64, 32, 128, 112
LOG2E = math.log2(math.e)
UNROLL = 8
VALUE = True
BFHID = False
SPLIT = 1
GT = 8

def radiate_kernel(prof_ref, cos_ref, alb_ref, wh_ref, wo_ref, sw_ref, heat_ref, surf_ref,
                   whb, wob, swb, hid, mass_s, k_s, opt, t_s, s_s, inv_s, n_s, d_s, net_s):
    C = prof_ref.shape[0]
    @pl.when(pl.program_id(0) == 0)
    def _():
        whb[...] = jnp.zeros_like(whb)
        wt = (wh_ref[...].astype(jnp.float32) * 0.5).T.astype(jnp.bfloat16)
        for j in range(8):
            whb[j*H:(j+1)*H, j*F:(j+1)*F] = wt
        r = lax.broadcasted_iota(jnp.int32, (16, 256), 0)
        c = lax.broadcasted_iota(jnp.int32, (16, 256), 1)
        whb[8*H:8*H+16, :] = jnp.where(c == r * F, 1.0, 0.0).astype(jnp.bfloat16)
        wo = wo_ref[...].astype(jnp.float32).T
        for g in range(0, G, 16):
            wob[3*g:3*g+16] = wo[g:g+16].astype(jnp.bfloat16)
            wob[3*g+16:3*g+32] = (wo[G+g:G+g+16] * 0.5).astype(jnp.bfloat16)
            wob[3*g+32:3*g+48] = wo[2*G+g:2*G+g+16].astype(jnp.bfloat16)
        swb[...] = jnp.broadcast_to(sw_ref[...], (C, G)).T
    cos = cos_ref[...].astype(jnp.float32)
    alb = alb_ref[...].astype(jnp.float32)
    scale = (-2.0 * LOG2E / L) / cos
    n_s[...] = jnp.broadcast_to(alb, (G, C))

    def chunk_body(i, _):
        ch = 7 - i
        x = prof_ref[:, pl.ds(pl.multiple_of(ch * 256, 256), 256)]
        pre = lax.dot_general(whb[...], x, (((1,), (1,)), ((), ())), preferred_element_type=jnp.float32)
        h = pre[:8*H]
        if BFHID:
            hb = h.astype(jnp.bfloat16)
            hid[...] = hb + hb * jnp.tanh(hb)
        else:
            hid[...] = (h + h * jnp.tanh(h)).astype(jnp.bfloat16)
        mass = pre[8*H:8*H+8]
        mass_s[pl.ds(pl.multiple_of(ch * 8, 8), 8), :] = mass
        kk = mass * scale
        for j in range(8):
            k_s[j] = jnp.broadcast_to(kk[j:j+1], (8, C))
        d_s[...] = jnp.ones((G, C), jnp.float32)

        def level(jj):
            l = ch * 8 + jj
            off = jj * H if isinstance(jj, int) else pl.multiple_of(jj * H, H)
            W = C // SPLIT
            for sp in range(SPLIT):
                cs = slice(sp * W, (sp + 1) * W)
                hl = hid[pl.ds(off, H), cs]
                o = jnp.dot(wob[...], hl, preferred_element_type=jnp.float32)
                if not VALUE:
                    opt[:, cs] = o
                    o = opt.at[:, cs]
                kl = k_s[jj, :, cs]
                if GT == 16: kl = jnp.concatenate([kl, kl], axis=0)
                for g in range(0, G, GT):
                    base = 3 * (g // 16) * 16 + g % 16
                    a = o[base:base+GT, :]
                    b = o[base+16:base+16+GT, :]
                    c = o[base+32:base+32+GT, :]
                    D = jnp.exp2(kl * jnp.exp2(a * LOG2E))
                    E = 1.0 - D
                    h2 = (0.245 + 0.245 * jnp.tanh(b)) * E
                    w = h2 * (0.8 * jnp.tanh(c))
                    r = h2 - w
                    t = D + (h2 + w)
                    N = n_s[g:g+GT, cs]
                    Dn = d_s[g:g+GT, cs] - r * N
                    Nn = r * Dn + t * (t * N)
                    n_s[g:g+GT, cs] = Nn
                    d_s[g:g+GT, cs] = Dn
                    t_s[l, g:g+GT, cs] = t
                    s_s[l, g:g+GT, cs] = Dn - Nn
        if UNROLL == 8:
            for jj in range(7, -1, -1): level(jj)
        else:
            def lb(j, _):
                for u in range(UNROLL):
                    level(7 - (j * UNROLL + u))
                return 0
            lax.fori_loop(0, 8 // UNROLL, lb, 0)
        for g in range(0, G, 8):
            inv = pltpu.reciprocal(d_s[g:g+8, :], approx=False)
            inv_s[ch, g:g+8, :] = inv
            n_s[g:g+8, :] = n_s[g:g+8, :] * inv
        return 0
    lax.fori_loop(0, 8, chunk_body, 0)

    W = 128
    for sp in range(C // W):
        cs = slice(sp * W, (sp + 1) * W)
        def down_chunk(ch, down):
            w = [down[i] * inv_s[ch, 8*i:8*i+8, cs] for i in range(G // 8)]
            rows = []
            for j in range(8):
                l = ch * 8 + j
                acc = None
                for i in range(G // 8):
                    p = w[i] * s_s[l, 8*i:8*i+8, cs]
                    acc = p if acc is None else acc + p
                    w[i] = w[i] * t_s[l, 8*i:8*i+8, cs]
                rows.append(jnp.sum(acc, axis=0, keepdims=True))
            net_s[pl.ds(pl.multiple_of(ch * 8, 8), 8), cs] = jnp.concatenate(rows, axis=0)
            return tuple(w)
        down = lax.fori_loop(0, 8, down_chunk, tuple(swb[g:g+8, cs] * cos[:, cs] for g in range(0, G, 8)))
        acc = down[0]
        for g in range(1, G//8):
            acc = acc + down[g]
        surf = jnp.sum(acc, axis=0, keepdims=True)
        surf_ref[:, cs] = surf
        net_s[L:L+1, cs] = surf * (1.0 - alb[:, cs])
    heat_ref[...] = L * (net_s[0:L, :] - net_s[1:L+1, :]) / mass_s[...]

def radiate(prof, cos, alb, wh, wo, sw, C=256):
    N = prof.shape[0]
    grid = (N // C,)
    full = lambda s: pl.BlockSpec(s, lambda i: (0,) * len(s))
    return pl.pallas_call(
        radiate_kernel,
        grid=grid,
        in_specs=[pl.BlockSpec((C, L*F), lambda i: (i, 0)),
                  pl.BlockSpec((1, C), lambda i: (0, i)),
                  pl.BlockSpec((1, C), lambda i: (0, i)),
                  full((F, H)), full((H, 3*G)), full((1, G))],
        out_specs=[pl.BlockSpec((L, C), lambda i: (0, i)), pl.BlockSpec((1, C), lambda i: (0, i))],
        out_shape=[jax.ShapeDtypeStruct((L, N), jnp.float32), jax.ShapeDtypeStruct((1, N), jnp.float32)],
        scratch_shapes=[pltpu.VMEM((8*H+16, 256), jnp.bfloat16), pltpu.VMEM((3*G, H), jnp.bfloat16), pltpu.VMEM((G, C), jnp.float32),
                        pltpu.VMEM((8*H, C), jnp.bfloat16), pltpu.VMEM((L, C), jnp.float32), pltpu.VMEM((8, 8, C), jnp.float32),
                        pltpu.VMEM((3*G, C), jnp.float32), pltpu.VMEM((L, G, C), jnp.float32), pltpu.VMEM((L, G, C), jnp.float32),
                        pltpu.VMEM((8, G, C), jnp.float32), pltpu.VMEM((G, C), jnp.float32), pltpu.VMEM((G, C), jnp.float32),
                        pltpu.VMEM((L+8, C), jnp.float32)],
        compiler_params=pltpu.CompilerParams(vmem_limit_bytes=60*2**20),
        cost_estimate=pl.CostEstimate(flops=6*10**9, bytes_accessed=2**23, transcendentals=4*10**7),
    )(prof, cos.reshape(1, N), alb.reshape(1, N), wh, wo, sw.reshape(1, G))


def mask_kernel(lists_ref, order_ref, raw_heat_ref, raw_surf_ref, heat_ref, surf_ref):
    devices, entries = lists_ref.shape
    columns = order_ref.shape[1]
    per_peer = columns // devices
    me = lax.axis_index("face") * lax.axis_size("tile") + lax.axis_index("tile")
    lists = lists_ref[...]
    ones = jnp.ones((8, entries), jnp.bfloat16)
    one_hot = lambda hit: jnp.where(hit, 1.0, 0.0).astype(jnp.bfloat16)
    contract_lanes = (((1,), (1,)), ((), ()))
    rows = []
    for k in range(per_peer):
        hit = one_hot(lists == me * per_peer + k)
        rows.append(lax.dot_general(ones, hit, contract_lanes, preferred_element_type=jnp.float32)[0:1])
    flags = jnp.concatenate(rows, axis=0)
    slot = lax.broadcasted_iota(jnp.int32, (devices, columns), 1)
    peer = lax.broadcasted_iota(jnp.int32, (devices, columns), 0)
    spread = jnp.dot(flags.astype(jnp.bfloat16), one_hot(slot // per_peer == peer), preferred_element_type=jnp.float32)
    share = lax.broadcasted_iota(jnp.int32, (per_peer, columns), 0)
    at = lax.broadcasted_iota(jnp.int32, (per_peer, columns), 1)
    flag = jnp.sum(jnp.where(at % per_peer == share, spread, 0.0), axis=0, keepdims=True)
    order = order_ref[...]
    group = lax.broadcasted_iota(jnp.int32, (columns // 128, columns), 0)
    lane = lax.broadcasted_iota(jnp.int32, (128, columns), 0)
    left = jnp.where(order // 128 == group, flag, 0.0).astype(jnp.bfloat16)
    listed = lax.dot_general(left, one_hot(order % 128 == lane), contract_lanes, preferred_element_type=jnp.float32)
    for i in range(columns // 128):
        cs = slice(i * 128, (i + 1) * 128)
        live = listed[i : i + 1, :] > 0.5
        heat_ref[:, cs] = jnp.where(live, raw_heat_ref[:, cs], 0.0)
        surf_ref[:, cs] = jnp.where(live, raw_surf_ref[:, cs], 0.0)


def on_device(profiles, sun_cos, albedo, span_order, keep_list, ship_list, ship_count, w_hidden, optical_weight, solar_weight):
    ship_live = jnp.arange(ship_list.shape[1])[None, :] < ship_count[:, None]
    named = jnp.concatenate([keep_list, jnp.where(ship_live, ship_list, -1)], axis=1)
    lists = lax.all_gather(named, ("face", "tile"), axis=0, tiled=True)
    raw_heat, raw_surf = radiate(profiles, sun_cos, albedo, w_hidden, optical_weight, solar_weight)
    heat, surf = pl.pallas_call(
        mask_kernel,
        out_shape=[jax.ShapeDtypeStruct(raw_heat.shape, jnp.float32), jax.ShapeDtypeStruct(raw_surf.shape, jnp.float32)],
        cost_estimate=pl.CostEstimate(flops=2**23, bytes_accessed=2**20, transcendentals=0),
    )(lists, span_order, raw_heat, raw_surf)
    return heat, surf.reshape(-1)


def solution(mesh):
    both = ("face", "tile")
    rows, flat = P(both, None), P(both)
    placed = (rows, flat, flat, rows, rows, rows, flat, P(), P(), P())
    return jax.shard_map(on_device, mesh=mesh, in_specs=placed, out_specs=(P(None, both), flat), check_vma=False)
```

time: 453 us -> 101 us (0.22)
  other arithmetic: 234 us -> 1.34 us
  local copies, waits for them, and re-layouts: 85.3 us -> 4.9 us
  waiting for transfers between devices: 60.7 us -> 0 us
  Pallas kernels: 0 us -> 54.2 us
  starting transfers between devices: 45.9 us -> 0 us
  blocking collectives: 0 us -> 38.7 us
  matrix products: 20.7 us -> 0 us
    dynamic_update_slice x64 -> x0, other arithmetic: 127 us -> none  [two_stream(): lax.scan(upward, ground, (reflect, transmit), reverse=True)]
    reduce_sum x65 -> x0, other arithmetic: 74.6 us -> none  [the longest x64 74.6 us: downward(): net_flux = jnp.sum(flux_down * (1.0 - reflect_here), axis=0)]
    all_to_all x5 -> x0, waiting for transfers between devices: 54.8 us -> none  [the longest x1 40.1 us: on_device(): lax.all_to_all(send_profile, ('face', 'tile'), split_axis=0, concat_axis=...]
    pallas_call x0 -> x2, Pallas kernels: none -> 54.2 us  [the longest x1 51.6 us: radiate(): pl.pallas_call(radiate_kernel, grid=grid, in_specs=[pl.BlockSpec((C, L *...]
    gather x9 -> x0, local copies, waits for them, and re-layouts: 44.4 us -> none  [the longest x1 11.6 us: on_device(): send_profile = profiles[slot_permutation].reshape(devices, per_peer, -1)]
    all_to_all x5 -> x0, starting transfers between devices: 39.3 us -> none  [the longest x1 11.5 us: on_device(): lax.all_to_all(send_cosine, ('face', 'tile'), split_axis=0, concat_axis=0...]
    all_gather x0 -> x1, blocking collectives: none -> 38.7 us  [on_device(): lists = lax.all_gather(named, ('face', 'tile'), axis=0, tiled=True)]
    add x1 -> x0, other arithmetic: 26.2 us -> none  [two_stream(): direct_beam + single_albedo * (1.0 - backscatter) * (1.0 - direct_beam)]
  transfers between devices with their start and end apart: 10 -> 0, of which waited for: 5 -> 0; matrix products, arithmetic and copies ran while one was open for 12% -> 0% of each run, Pallas kernels for 0% -> 0%
where the time goes in v1:
time: 101 us; the launch traced here: 100 us
  Pallas kernels  54.2 us (54%)
  blocking collectives  38.7 us (38%)
  local copies, waits for them, and re-layouts  4.9 us (5%)
  other arithmetic  1.34 us (1%)
  between operations  1.28 us (1%)
    pallas_call x1, Pallas kernels, radiate(): pl.pallas_call(radiate_kernel, grid=grid, in_specs=[pl.BlockSpec((C, L *...  51.6 us
    all_gather x1, blocking collectives, on_device(): lists = lax.all_gather(named, ('face', 'tile'), axis=0, tiled=True)  38.7 us
    pallas_call x1, Pallas kernels, on_device(): pl.pallas_call(mask_kernel, out_shape=[jax.ShapeDtypeStruct(raw_heat.shap...  2.58 us
    unnamed x2, local copies, waits for them, and re-layouts  2.34 us

profile of v1, /device:TPU:1, one launch (start us, length us, event | category | flops | bytes accessed | tf_op | source)
XLA Modules:
  0.0 100.4 jit_solution(3728553969274808888)
XLA Ops:
  1.3 0.7 compare_select_fusion
  1.9 0.7 add_bitcast_fusion
  2.6 1.3 %reshape.27.cos_ref = bf16[1,1024]{1,0:T(2,128)(2,1)} reshape(bf16[1024]{0:T(1024)(128)(2,1)} %param.11) | data formatting | bytes 4096 | tf_op jit(solution)/shard_map/reshape | solution.py:147
  3.9 1.3 %reshape.28.alb_ref = bf16[1,1024]{1,0:T(2,128)(2,1)} reshape(bf16[1024]{0:T(1024)(128)(2,1)} %param.12) | data formatting | bytes 4096 | tf_op jit(solution)/shard_map/reshape | solution.py:147
  5.2 1.6 %copy.13.wo_ref = bf16[128,336]{1,0:T(8,128)(2,1)} copy(bf16[128,336]{0,1:T(8,128)(2,1)} %param.18) | data formatting | bytes 172032 | tf_op args[8]
  6.8 51.6 %shard_map.113 = (f32[64,1024]{1,0:T(8,128)}, f32[1,1024]{1,0:T(1,128)}) custom-call(bf16[1024,2048]{1,0:T(8,128)(2,1)} %prof_ref.1, bf16[1,1024]{1,0:T(2,128)(2,1)} %reshape.27.cos_ref, bf16[1,1024]{1,0:T(2,128)(2,1)} %reshape.28.alb_ref, bf16[32,128]{1,0:T(8,128)(2,1)} %wh_ref.1, bf16[128,336]{1,0:T(8,128)(2,1)} %copy.13.wo_ref, f32[1,112]{1,0:T(1,128)} %bitcast.11), custom_call_target="tpu_custom_call" | custom-call | flops 6000000000 | bytes 8388608 | tf_op jit(solution)/shard_map/pallas_call | solution.py:131
  58.4 38.7 %all-gather = s32[128,1,512]{2,1,0:T(1,128)S(1)} all-gather(s32[1,1,512]{2,1,0:T(1,128)S(1)} %add_bitcast_fusion), channel_id=1, replica_groups=mesh['face'=4,'tile'=32] {'face','tile'}, dimensions={0}, use_global_device_ids=true | all-gather | bytes 264192 | tf_op jit(solution)/shard_map/all_gather | solution.py:185
  97.1 0.7 copy.16
  97.8 2.6 %shard_map.114 = (f32[64,1024]{1,0:T(8,128)}, f32[1,1024]{1,0:T(1,128)}) custom-call(s32[128,512]{1,0:T(8,128)} %bitcast.9, s32[1,1024]{1,0:T(1,128)} %order_ref.1, f32[64,1024]{1,0:T(8,128)} %get-tuple-element.6.raw_heat_ref, f32[1,1024]{1,0:T(1,128)} %get-tuple-element.7.raw_surf_ref), custom_call_target="tpu_custom_call" | custom-call | flops 8388608 | bytes 1048576 | tf_op jit(solution)/shard_map/pallas_call | solution.py:187

commit v2 on v1

v2 whole, which is shorter than its diff:
```python
import functools, math
import jax, jax.numpy as jnp
from jax import lax
from jax.experimental import pallas as pl
from jax.experimental.pallas import tpu as pltpu
from jax.sharding import PartitionSpec as P

L, F, H, G = 64, 32, 128, 112
LOG2E = math.log2(math.e)
U = 4
W = 256
DU = 1
ORDER = 0
NODOT = False
STAGE = False
XT = 0
NH = 8
NG = 8
ND = 8
DFIRST = False
RENORM = 8

def radiate_kernel(prof_ref, cos_ref, alb_ref, wh_ref, wo_ref, sw_ref, heat_ref, surf_ref,
                   whb, wob, swb, hid, mass_s, k_s, opt, t_s, s_s, inv_s, n_s, d_s, net_s):
    C = prof_ref.shape[0]
    @pl.when(pl.program_id(0) == 0)
    def _():
        whb[...] = jnp.zeros_like(whb)
        wt = (wh_ref[...].astype(jnp.float32) * 0.5).T.astype(jnp.bfloat16)
        for j in range(8):
            whb[j*H:(j+1)*H, j*F:(j+1)*F] = wt
        r = lax.broadcasted_iota(jnp.int32, (16, 256), 0)
        c = lax.broadcasted_iota(jnp.int32, (16, 256), 1)
        whb[8*H:8*H+16, :] = jnp.where(c == r * F, 1.0, 0.0).astype(jnp.bfloat16)
        for g in range(0, G, 16):
            wob[3*g:3*g+16] = wo_ref[g:g+16]
            wob[3*g+16:3*g+32] = (wo_ref[G+g:G+g+16].astype(jnp.float32) * 0.5).astype(jnp.bfloat16)
            wob[3*g+32:3*g+48] = wo_ref[2*G+g:2*G+g+16]
        swb[...] = jnp.broadcast_to(sw_ref[...], (128, G)).T
    cos = cos_ref[...].astype(jnp.float32)
    alb = alb_ref[...].astype(jnp.float32)
    scale = (-2.0 * LOG2E / L) / cos
    n_s[...] = jnp.broadcast_to(alb, (G, C))

    def hidden_chunk(ch, _):
        k0 = pl.multiple_of(ch * 256, 256)
        for s in range(C // W):
            cs = slice(s * W, (s + 1) * W)
            x = prof_ref[cs, pl.ds(k0, 256)]
            if XT == 0:
                pre = lax.dot_general(whb[...], x, (((1,), (1,)), ((), ())), preferred_element_type=jnp.float32)
            elif XT == 1:
                pre = jnp.dot(whb[...], x.T, preferred_element_type=jnp.float32)
            elif XT == 2:
                pre = jnp.dot(whb[...], x.astype(jnp.float32).T.astype(jnp.bfloat16), preferred_element_type=jnp.float32)
            h = pre[:8*H]
            hid[pl.ds(pl.multiple_of(ch * 8 * H, 8 * H), 8 * H), cs] = (h + h * jnp.tanh(h)).astype(jnp.bfloat16)
            mass = pre[8*H:8*H+8]
            mass_s[pl.ds(pl.multiple_of(ch * 8, 8), 8), cs] = mass
            kk = mass * scale[:, cs]
            for j in range(8):
                k_s[ch * 8 + j, :, cs] = jnp.broadcast_to(kk[j:j+1], (8, W))
        return 0
    lax.fori_loop(0, NH, hidden_chunk, 0)

    def dots(l, p):
        for u in range(U):
            for s in range(C // W):
                cs = slice(s * W, (s + 1) * W)
                lu = jnp.maximum(l - u, 0)
                opt[p, u, :, cs] = jnp.dot(wob[...], hid[pl.ds(pl.multiple_of(lu * H, H), H), cs], preferred_element_type=jnp.float32)

    def elem(l, p):
        for s in range(C // 128):
            cs = slice(s * 128, (s + 1) * 128)
            for g in range(0, G, 8):
                base = 3 * (g // 16) * 16 + g % 16
                N = n_s[g:g+8, cs]
                Dn = d_s[g:g+8, cs]
                for u in range(U):
                    a = opt[p, u, base:base+8, cs]
                    b = opt[p, u, base+16:base+24, cs]
                    c = opt[p, u, base+32:base+40, cs]
                    D = jnp.exp2(k_s[l - u, :, cs] * jnp.exp2(a * LOG2E))
                    E = 1.0 - D
                    h2 = (0.245 + 0.245 * jnp.tanh(b)) * E
                    w = h2 * (0.8 * jnp.tanh(c))
                    r = h2 - w
                    t = D + (h2 + w)
                    Dn = Dn - r * N
                    N = r * Dn + t * (t * N)
                    t_s[l - u, g:g+8, cs] = t
                    s_s[l - u, g:g+8, cs] = Dn - N
                n_s[g:g+8, cs] = N
                d_s[g:g+8, cs] = Dn

    dots(L - 1, 0)
    def group(i, _):
        l0 = L - 1 - i * RENORM
        d_s[...] = jnp.ones((G, C), jnp.float32)
        def inner(j, _):
            l = l0 - U * j
            for p in (0, 1):
                @pl.when(lax.rem(j, 2) == p)
                def _():
                    if DFIRST:
                        NODOT or dots(l - U, 1 - p)
                        elem(l, p)
                    else:
                        elem(l, p)
                        NODOT or dots(l - U, 1 - p)
            return 0
        lax.fori_loop(0, RENORM // U, inner, 0)
        ch = L // RENORM - 1 - i
        for g in range(0, G, 8):
            inv = pltpu.reciprocal(d_s[g:g+8, :], approx=False)
            inv_s[ch, g:g+8, :] = inv
            n_s[g:g+8, :] = n_s[g:g+8, :] * inv
        return 0
    lax.fori_loop(0, NG * (8 // RENORM), group, 0)

    V = 128
    for sp in range(C // V):
        cs = slice(sp * V, (sp + 1) * V)
        def down_chunk(ch, down):
            w = list(down)
            rows = []
            for j in range(8):
                l = ch * 8 + j
                if j % RENORM == 0:
                    ii = ch if RENORM == 8 else ch * (8 // RENORM) + j // RENORM
                    w = [w[i] * inv_s[ii, 8*i:8*i+8, cs] for i in range(G // 8)]
                acc = None
                for i in range(G // 8):
                    p = w[i] * s_s[l, 8*i:8*i+8, cs]
                    acc = p if acc is None else acc + p
                    w[i] = w[i] * t_s[l, 8*i:8*i+8, cs]
                rows.append(jnp.sum(acc, axis=0, keepdims=True))
            net_s[pl.ds(pl.multiple_of(ch * 8, 8), 8), cs] = jnp.concatenate(rows, axis=0)
            return tuple(w)
        down = lax.fori_loop(0, ND, down_chunk, tuple(swb[g:g+8, :] * cos[:, cs] for g in range(0, G, 8)))
        acc = down[0]
        for g in range(1, G//8):
            acc = acc + down[g]
        surf = jnp.sum(acc, axis=0, keepdims=True)
        surf_ref[:, cs] = surf
        net_s[L:L+1, cs] = surf * (1.0 - alb[:, cs])
    heat_ref[...] = L * (net_s[0:L, :] - net_s[1:L+1, :]) / mass_s[...]

def radiate(prof, cos, alb, wh, wo, sw, C=256):
    N = prof.shape[0]
    grid = (N // C,)
    full = lambda s: pl.BlockSpec(s, lambda i: (0,) * len(s))
    vm = lambda *s: pltpu.VMEM(s, jnp.float32)
    vb = lambda *s: pltpu.VMEM(s, jnp.bfloat16)
    return pl.pallas_call(
        radiate_kernel,
        grid=grid,
        in_specs=[pl.BlockSpec((C, L*F), lambda i: (i, 0)),
                  pl.BlockSpec((1, C), lambda i: (0, i)),
                  pl.BlockSpec((1, C), lambda i: (0, i)),
                  full((F, H)), full((3*G, H)), full((1, G))],
        out_specs=[pl.BlockSpec((L, C), lambda i: (0, i)), pl.BlockSpec((1, C), lambda i: (0, i))],
        out_shape=[jax.ShapeDtypeStruct((L, N), jnp.float32), jax.ShapeDtypeStruct((1, N), jnp.float32)],
        scratch_shapes=[vb(8*H+16, 256), vb(3*G, H), vm(G, 128), vb(L*H, C), vm(L, C), vm(L, 8, C),
                        vm(2, U, 3*G, C), vm(L, G, C), vm(L, G, C), vm(L // RENORM, G, C), vm(G, C), vm(G, C), vm(L+8, C)],
        compiler_params=pltpu.CompilerParams(vmem_limit_bytes=60*2**20),
        cost_estimate=pl.CostEstimate(flops=6*10**9, bytes_accessed=2**23, transcendentals=4*10**7),
    )(prof, cos, alb, wh, wo.T, sw.reshape(1, G))


def prepare_kernel(cos_ref, alb_ref, keep_ref, ship_ref, count_ref, flags_ref, cos_row_ref, alb_row_ref):
    cos_row_ref[...] = cos_ref[...].astype(jnp.float32).reshape(cos_row_ref.shape)
    alb_row_ref[...] = alb_ref[...].astype(jnp.float32).reshape(alb_row_ref.shape)
    per_peer = flags_ref.shape[0]
    peers = flags_ref.shape[1] // 2
    one_hot = lambda hit: jnp.where(hit, 1.0, 0.0).astype(jnp.bfloat16)
    total = None
    for ref, live_count in ((keep_ref, keep_ref.shape[1]), (ship_ref, count_ref[0])):
        slots = ref[...]
        n = slots.shape[1]
        at = lax.broadcasted_iota(jnp.int32, (per_peer, n), 1)
        share = lax.broadcasted_iota(jnp.int32, (per_peer, n), 0)
        left = one_hot((slots % per_peer == share) & (at < live_count))
        right = one_hot(slots // per_peer == lax.broadcasted_iota(jnp.int32, (peers, n), 0))
        part = lax.dot_general(left, right, (((1,), (1,)), ((), ())), preferred_element_type=jnp.float32)
        total = part if total is None else total + part
    flags_ref[:, :peers] = total
    flags_ref[:, peers:] = jnp.zeros((per_peer, peers), jnp.float32)


def mask_kernel(flags_ref, order_ref, raw_heat_ref, raw_surf_ref, heat_ref, surf_ref):
    columns, peers = flags_ref.shape
    me = lax.axis_index("face") * lax.axis_size("tile") + lax.axis_index("tile")
    one_hot = lambda hit: jnp.where(hit, 1.0, 0.0).astype(jnp.bfloat16)
    contract_lanes = (((1,), (1,)), ((), ()))
    mine = one_hot(lax.broadcasted_iota(jnp.int32, (8, peers), 1) == me)
    flag = lax.dot_general(mine, flags_ref[...].astype(jnp.bfloat16), contract_lanes, preferred_element_type=jnp.float32)
    order = order_ref[...]
    group = lax.broadcasted_iota(jnp.int32, (columns // 128, columns), 0)
    lane = lax.broadcasted_iota(jnp.int32, (128, columns), 0)
    left = jnp.where(order // 128 == group, flag, 0.0).astype(jnp.bfloat16)
    listed = lax.dot_general(left, one_hot(order % 128 == lane), contract_lanes, preferred_element_type=jnp.float32)
    for i in range(columns // 128):
        cs = slice(i * 128, (i + 1) * 128)
        live = listed[i : i + 1, :] > 0.5
        heat_ref[:, cs] = jnp.where(live, raw_heat_ref[:, cs], 0.0)
        surf_ref[:, cs] = jnp.where(live, raw_surf_ref[:, cs], 0.0)


def on_device(profiles, sun_cos, albedo, span_order, keep_list, ship_list, ship_count, w_hidden, optical_weight, solar_weight):
    columns = profiles.shape[0]
    devices = lax.axis_size(("face", "tile"))
    per_peer = columns // devices
    f32 = lambda *s: jax.ShapeDtypeStruct(s, jnp.float32)
    vmem = pl.BlockSpec(memory_space=pltpu.VMEM)
    flags, cos_row, alb_row = pl.pallas_call(
        prepare_kernel,
        in_specs=[vmem] * 4 + [pl.BlockSpec(memory_space=pltpu.SMEM)],
        out_specs=[vmem] * 3,
        out_shape=[f32(per_peer, 2 * devices), f32(1, columns), f32(1, columns)],
        cost_estimate=pl.CostEstimate(flops=2**20, bytes_accessed=2**14, transcendentals=0),
    )(sun_cos, albedo, keep_list, ship_list, ship_count)
    gathered = lax.all_gather(flags, ("face", "tile"), axis=0, tiled=True)
    raw_heat, raw_surf = radiate(profiles, cos_row, alb_row, w_hidden, optical_weight, solar_weight)
    first = pl.BlockSpec((columns, devices), lambda i: (0, 0))
    whole = lambda *s: pl.BlockSpec(s, lambda i: (0, 0))
    heat, surf = pl.pallas_call(
        mask_kernel,
        grid=(1,),
        in_specs=[first, whole(1, columns), whole(*raw_heat.shape), whole(1, columns)],
        out_specs=[whole(*raw_heat.shape), whole(1, columns)],
        out_shape=[f32(*raw_heat.shape), f32(1, columns)],
        cost_estimate=pl.CostEstimate(flops=2**23, bytes_accessed=2**20, transcendentals=0),
    )(gathered, span_order, raw_heat, raw_surf)
    return heat, surf.reshape(-1)


def solution(mesh):
    both = ("face", "tile")
    rows, flat = P(both, None), P(both)
    placed = (rows, flat, flat, rows, rows, rows, flat, P(), P(), P())
    return jax.shard_map(on_device, mesh=mesh, in_specs=placed, out_specs=(P(None, both), flat), check_vma=False)
```

time: 101 us -> 87.8 us (0.87)
  blocking collectives: 38.7 us -> 0 us
  waiting for transfers between devices: 0 us -> 21.9 us
  between operations: 1.28 us -> 14.7 us
  local copies, waits for them, and re-layouts: 4.9 us -> 0 us
  Pallas kernels: 54.2 us -> 51 us
  other arithmetic: 1.34 us -> 0 us
    all_gather x1 -> x0, blocking collectives: 38.7 us -> none  [on_device(): lists = lax.all_gather(named, ('face', 'tile'), axis=0, tiled=True)]
    all_gather x0 -> x1, waiting for transfers between devices: none -> 21.9 us  [on_device(): gathered = lax.all_gather(flags, ('face', 'tile'), axis=0, tiled=True)]
    pallas_call x1, Pallas kernels: 51.6 us -> 47.3 us  [radiate(): pl.pallas_call(radiate_kernel, grid=grid, in_specs=[pl.BlockSpec((C, L *...]
    reshape x2 -> x0, local copies, waits for them, and re-layouts: 2.55 us -> none  [the longest x1 1.28 us: radiate(): alb.reshape(1, N)]
    unnamed x2 -> x0, local copies, waits for them, and re-layouts: 2.34 us -> none
    pallas_call x1 -> x2, Pallas kernels: 2.58 us -> 3.73 us  [the longest x1 2.22 us: on_device(): pl.pallas_call(mask_kernel, grid=(1,), in_specs=[first, whole(1, columns)...]
  transfers between devices with their start and end apart: 0 -> 1, of which waited for: 0 -> 1; matrix products, arithmetic and copies ran while one was open for 0% -> 0% of each run, Pallas kernels for 0% -> 54%
where the time goes in v2:
time: 87.8 us; the launch traced here: 87.6 us
  Pallas kernels  51 us (58%)
  waiting for transfers between devices  21.9 us (25%)
  between operations  14.7 us (17%)
    pallas_call x1, Pallas kernels, radiate(): pl.pallas_call(radiate_kernel, grid=grid, in_specs=[pl.BlockSpec((C, L *...  47.3 us
    all_gather x1, waiting for transfers between devices, on_device(): gathered = lax.all_gather(flags, ('face', 'tile'), axis=0, tiled=True)  21.9 us
    pallas_call x1, Pallas kernels, on_device(): pl.pallas_call(mask_kernel, grid=(1,), in_specs=[first, whole(1, columns)...  2.22 us
  transfers between devices with their start and end apart: 1, of which 1 were waited for; matrix products, arithmetic and copies ran while one was open for 0% of the time, Pallas kernels for 54%

profile of v2, /device:TPU:1, one launch (start us, length us, event | category | flops | bytes accessed | tf_op | source)
XLA Modules:
  0.0 87.6 jit_solution(9282662050826061030)
XLA Ops:
  7.2 0.0 all-gather.2.cloned.1.call-start
  7.9 1.5 %shard_map.113 = (f32[8,256]{1,0:T(8,128)}, f32[1,1024]{1,0:T(1,128)}, f32[1,1024]{1,0:T(1,128)}) custom-call(bf16[1024]{0:T(1024)(128)(2,1)} %cos_ref.1, bf16[1024]{0:T(1024)(128)(2,1)} %alb_ref.1, s32[1,384]{1,0:T(1,128)} %keep_ref.1, s32[1,128]{1,0:T(1,128)} %ship_ref.1, s32[1]{0:T(128)S(6)} %copy.12.count_ref), custom_call_target="tpu_custom_call" | custom-call | flops 1048576 | bytes 16384 | tf_op jit(solution)/shard_map/pallas_call | solution.py:217
  9.4 0.0 all-gather.2.cloned.1.call-update
  9.4 47.3 %shard_map.114 = (f32[64,1024]{1,0:T(8,128)}, f32[1,1024]{1,0:T(1,128)}) custom-call(bf16[1024,2048]{1,0:T(8,128)(2,1)} %prof_ref.1, f32[1,1024]{1,0:T(1,128)} %get-tuple-element.10.cos_ref, f32[1,1024]{1,0:T(1,128)} %get-tuple-element.11.alb_ref, bf16[32,128]{1,0:T(8,128)(2,1)} %wh_ref.1, bf16[336,128]{1,0:T(8,128)(2,1)} %bitcast.3, f32[1,112]{1,0:T(1,128)} %bitcast.5), custom_call_target="tpu_custom_call" | custom-call | flops 6000000000 | bytes 8388608 | tf_op jit(solution)/shard_map/pallas_call | solution.py:156
  56.7 21.9 %all-gather.2.cloned.1.call-done.flags_ref = f32[1024,256]{1,0:T(8,128)} async-done(((f32[8,256]{1,0:T(8,128)}), f32[1024,256]{1,0:T(8,128)}) %all-gather.2.cloned.1.call-update) | async-done | bytes 1048592 | tf_op jit(solution)/shard_map/all_gather | solution.py:224
  78.6 2.2 %shard_map.115 = (f32[64,1024]{1,0:T(8,128)}, f32[1,1024]{1,0:T(1,128)}) custom-call(f32[1024,256]{1,0:T(8,128)} %all-gather.2.cloned.1.call-done.flags_ref, s32[1,1024]{1,0:T(1,128)} %order_ref.1, f32[64,1024]{1,0:T(8,128)} %get-tuple-element.12.raw_heat_ref, f32[1,1024]{1,0:T(1,128)} %get-tuple-element.13.raw_surf_ref), custom_call_target="tpu_custom_call" | custom-call | flops 8388608 | bytes 1048576 | tf_op jit(solution)/shard_map/pallas_call | solution.py:228
Async XLA Ops:
  7.2 71.4 %all-gather.2.cloned.1.call-start = ((), (), s32[]{:S(2)}) async-start(), calls=%async_computation | async-start | bytes 1056768 | tf_op jit(solution)/shard_map/all_gather | solution.py:224
Sparse Core Ops, SparseCore 0:
  11.4 67.1 all-gather.1

commit v3 on v2

--- a/solution.py
+++ b/solution.py
@@ -20,7 +20,7 @@
 DFIRST = False
 RENORM = 8
 
-def radiate_kernel(prof_ref, cos_ref, alb_ref, wh_ref, wo_ref, sw_ref, heat_ref, surf_ref,
+def radiate_kernel(prof_ref, cos_ref, alb_ref, live_ref, wh_ref, wo_ref, sw_ref, heat_ref, surf_ref,
                    whb, wob, swb, hid, mass_s, k_s, opt, t_s, s_s, inv_s, n_s, d_s, net_s):
     C = prof_ref.shape[0]
     @pl.when(pl.program_id(0) == 0)
@@ -143,11 +143,12 @@
         for g in range(1, G//8):
             acc = acc + down[g]
         surf = jnp.sum(acc, axis=0, keepdims=True)
-        surf_ref[:, cs] = surf
+        surf_ref[:, cs] = jnp.where(live_ref[:, cs] > 0.5, surf, 0.0)
         net_s[L:L+1, cs] = surf * (1.0 - alb[:, cs])
-    heat_ref[...] = L * (net_s[0:L, :] - net_s[1:L+1, :]) / mass_s[...]
-
-def radiate(prof, cos, alb, wh, wo, sw, C=256):
+    live = live_ref[...] > 0.5
+    heat_ref[...] = jnp.where(live, L * (net_s[0:L, :] - net_s[1:L+1, :]) / mass_s[...], 0.0)
+
+def radiate(prof, cos, alb, live, wh, wo, sw, C=256):
     N = prof.shape[0]
     grid = (N // C,)
     full = lambda s: pl.BlockSpec(s, lambda i: (0,) * len(s))
@@ -159,6 +160,7 @@
         in_specs=[pl.BlockSpec((C, L*F), lambda i: (i, 0)),
                   pl.BlockSpec((1, C), lambda i: (0, i)),
                   pl.BlockSpec((1, C), lambda i: (0, i)),
+                  pl.BlockSpec((1, C), lambda i: (0, i)),
                   full((F, H)), full((3*G, H)), full((1, G))],
         out_specs=[pl.BlockSpec((L, C), lambda i: (0, i)), pl.BlockSpec((1, C), lambda i: (0, i))],
         out_shape=[jax.ShapeDtypeStruct((L, N), jnp.float32), jax.ShapeDtypeStruct((1, N), jnp.float32)],
@@ -166,73 +168,111 @@
                         vm(2, U, 3*G, C), vm(L, G, C), vm(L, G, C), vm(L // RENORM, G, C), vm(G, C), vm(G, C), vm(L+8, C)],
         compiler_params=pltpu.CompilerParams(vmem_limit_bytes=60*2**20),
         cost_estimate=pl.CostEstimate(flops=6*10**9, bytes_accessed=2**23, transcendentals=4*10**7),
-    )(prof, cos, alb, wh, wo.T, sw.reshape(1, G))
-
-
-def prepare_kernel(cos_ref, alb_ref, keep_ref, ship_ref, count_ref, flags_ref, cos_row_ref, alb_row_ref):
+    )(prof, cos, alb, live, wh, wo.T, sw.reshape(1, G))
+
+
+LO, HI = 16, 8
+
+
+def listed_kernel(cos_ref, alb_ref, keep_ref, ship_ref, count_ref, order_ref, cos_row_ref, alb_row_ref, live_ref,
+                  made, first, turned, second, send1, recv1, send2, recv2):
+    per_peer = order_ref.shape[1] // (LO * HI)
+    columns = order_ref.shape[1]
+    devices = LO * HI
+    tiles = lax.axis_size("tile")
+    me = lax.axis_index("face") * tiles + lax.axis_index("tile")
+    hi, lo = me // LO, me % LO
+
+    def place(h, l):
+        device = h * LO + l
+        return (device // tiles, device % tiles)
+
+    barrier = pltpu.get_barrier_semaphore()
+    for j in range(1, LO):
+        pl.semaphore_signal(barrier, inc=1, device_id=place(hi, (lo + j) % LO), device_id_type=pl.DeviceIdType.MESH)
+    for j in range(1, HI):
+        pl.semaphore_signal(barrier, inc=1, device_id=place((hi + j) % HI, lo), device_id_type=pl.DeviceIdType.MESH)
+
     cos_row_ref[...] = cos_ref[...].astype(jnp.float32).reshape(cos_row_ref.shape)
     alb_row_ref[...] = alb_ref[...].astype(jnp.float32).reshape(alb_row_ref.shape)
-    per_peer = flags_ref.shape[0]
-    peers = flags_ref.shape[1] // 2
     one_hot = lambda hit: jnp.where(hit, 1.0, 0.0).astype(jnp.bfloat16)
+    lanes = (((1,), (1,)), ((), ()))
     total = None
-    for ref, live_count in ((keep_ref, keep_ref.shape[1]), (ship_ref, count_ref[0])):
+    for ref, live_count in ((keep_ref, keep_ref.shape[1]), (ship_ref, count_ref[...])):
         slots = ref[...]
         n = slots.shape[1]
-        at = lax.broadcasted_iota(jnp.int32, (per_peer, n), 1)
-        share = lax.broadcasted_iota(jnp.int32, (per_peer, n), 0)
-        left = one_hot((slots % per_peer == share) & (at < live_count))
-        right = one_hot(slots // per_peer == lax.broadcasted_iota(jnp.int32, (peers, n), 0))
-        part = lax.dot_general(left, right, (((1,), (1,)), ((), ())), preferred_element_type=jnp.float32)
+        row = lax.broadcasted_iota(jnp.int32, (devices, n), 0)
+        at = lax.broadcasted_iota(jnp.int32, (devices, n), 1)
+        peer = (row % HI) * LO + row // HI
+        left = one_hot(slots // per_peer == peer)
+        right = one_hot((slots % per_peer == row) & (at < live_count))
+        part = lax.dot_general(left, right, lanes, preferred_element_type=jnp.float32)
         total = part if total is None else total + part
-    flags_ref[:, :peers] = total
-    flags_ref[:, peers:] = jnp.zeros((per_peer, peers), jnp.float32)
-
-
-def mask_kernel(flags_ref, order_ref, raw_heat_ref, raw_surf_ref, heat_ref, surf_ref):
-    columns, peers = flags_ref.shape
-    me = lax.axis_index("face") * lax.axis_size("tile") + lax.axis_index("tile")
-    one_hot = lambda hit: jnp.where(hit, 1.0, 0.0).astype(jnp.bfloat16)
-    contract_lanes = (((1,), (1,)), ((), ()))
-    mine = one_hot(lax.broadcasted_iota(jnp.int32, (8, peers), 1) == me)
-    flag = lax.dot_general(mine, flags_ref[...].astype(jnp.bfloat16), contract_lanes, preferred_element_type=jnp.float32)
+    made[...] = total.reshape(LO, HI, 128)
+
+    pl.semaphore_wait(barrier, LO + HI - 2)
+    copies = []
+    for j in range(1, LO):
+        to = (lo + j) % LO
+        copy = pltpu.make_async_remote_copy(
+            src_ref=made.at[to], dst_ref=first.at[lo], send_sem=send1.at[j], recv_sem=recv1.at[j],
+            device_id=place(hi, to), device_id_type=pl.DeviceIdType.MESH)
+        copy.start()
+        copies.append(copy)
+    first[lo] = made[lo]
+    for copy in copies:
+        copy.wait()
+    turned[...] = jnp.swapaxes(first[...], 0, 1)
+    copies = []
+    for j in range(1, HI):
+        to = (hi + j) % HI
+        copy = pltpu.make_async_remote_copy(
+            src_ref=turned.at[to], dst_ref=second.at[hi], send_sem=send2.at[j], recv_sem=recv2.at[j],
+            device_id=place(to, lo), device_id_type=pl.DeviceIdType.MESH)
+        copy.start()
+        copies.append(copy)
+    second[hi] = turned[hi]
+    for copy in copies:
+        copy.wait()
+
+    got = second[...].reshape(devices, 128).astype(jnp.bfloat16)
+    pick = one_hot(lax.broadcasted_iota(jnp.int32, (per_peer, 128), 0) == lax.broadcasted_iota(jnp.int32, (per_peer, 128), 1))
+    flags = lax.dot_general(pick, got, lanes, preferred_element_type=jnp.float32).astype(jnp.bfloat16)
+    span = lax.broadcasted_iota(jnp.int32, (devices, columns), 0)
+    at = lax.broadcasted_iota(jnp.int32, (devices, columns), 1)
+    spread = jnp.dot(flags, one_hot(at // per_peer == span), preferred_element_type=jnp.float32)
+    share = lax.broadcasted_iota(jnp.int32, (per_peer, columns), 0)
+    at8 = lax.broadcasted_iota(jnp.int32, (per_peer, columns), 1)
+    flag = jnp.sum(jnp.where(at8 % per_peer == share, spread, 0.0), axis=0, keepdims=True)
     order = order_ref[...]
     group = lax.broadcasted_iota(jnp.int32, (columns // 128, columns), 0)
     lane = lax.broadcasted_iota(jnp.int32, (128, columns), 0)
-    left = jnp.where(order // 128 == group, flag, 0.0).astype(jnp.bfloat16)
-    listed = lax.dot_general(left, one_hot(order % 128 == lane), contract_lanes, preferred_element_type=jnp.float32)
+    placed = jnp.where(order // 128 == group, flag, 0.0).astype(jnp.bfloat16)
+    listed = lax.dot_general(placed, one_hot(order % 128 == lane), lanes, preferred_element_type=jnp.float32)
     for i in range(columns // 128):
-        cs = slice(i * 128, (i + 1) * 128)
-        live = listed[i : i + 1, :] > 0.5
-        heat_ref[:, cs] = jnp.where(live, raw_heat_ref[:, cs], 0.0)
-        surf_ref[:, cs] = jnp.where(live, raw_surf_ref[:, cs], 0.0)
+        live_ref[:, i * 128 : (i + 1) * 128] = listed[i : i + 1, :]
+
+
+def find_listed(sun_cos, albedo, keep_list, ship_list, ship_count, span_order):
+    columns = sun_cos.shape[0]
+    row = jax.ShapeDtypeStruct((1, columns), jnp.float32)
+    vmem = pl.BlockSpec(memory_space=pltpu.VMEM)
+    dma = pltpu.SemaphoreType.DMA
+    vm = lambda *s: pltpu.VMEM(s, jnp.float32)
+    return pl.pallas_call(
+        listed_kernel,
+        in_specs=[vmem] * 6,
+        out_specs=[vmem] * 3,
+        out_shape=[row] * 3,
+        scratch_shapes=[vm(LO, HI, 128), vm(LO, HI, 128), vm(HI, LO, 128), vm(HI, LO, 128), dma((LO,)), dma((LO,)), dma((HI,)), dma((HI,))],
+        compiler_params=pltpu.CompilerParams(collective_id=0, has_side_effects=True),
+        cost_estimate=pl.CostEstimate(flops=2**23, bytes_accessed=2**17, transcendentals=0),
+    )(sun_cos, albedo, keep_list, ship_list, ship_count.reshape(1, 1), span_order)
 
 
 def on_device(profiles, sun_cos, albedo, span_order, keep_list, ship_list, ship_count, w_hidden, optical_weight, solar_weight):
-    columns = profiles.shape[0]
-    devices = lax.axis_size(("face", "tile"))
-    per_peer = columns // devices
-    f32 = lambda *s: jax.ShapeDtypeStruct(s, jnp.float32)
-    vmem = pl.BlockSpec(memory_space=pltpu.VMEM)
-    flags, cos_row, alb_row = pl.pallas_call(
-        prepare_kernel,
-        in_specs=[vmem] * 4 + [pl.BlockSpec(memory_space=pltpu.SMEM)],
-        out_specs=[vmem] * 3,
-        out_shape=[f32(per_peer, 2 * devices), f32(1, columns), f32(1, columns)],
-        cost_estimate=pl.CostEstimate(flops=2**20, bytes_accessed=2**14, transcendentals=0),
-    )(sun_cos, albedo, keep_list, ship_list, ship_count)
-    gathered = lax.all_gather(flags, ("face", "tile"), axis=0, tiled=True)
-    raw_heat, raw_surf = radiate(profiles, cos_row, alb_row, w_hidden, optical_weight, solar_weight)
-    first = pl.BlockSpec((columns, devices), lambda i: (0, 0))
-    whole = lambda *s: pl.BlockSpec(s, lambda i: (0, 0))
-    heat, surf = pl.pallas_call(
-        mask_kernel,
-        grid=(1,),
-        in_specs=[first, whole(1, columns), whole(*raw_heat.shape), whole(1, columns)],
-        out_specs=[whole(*raw_heat.shape), whole(1, columns)],
-        out_shape=[f32(*raw_heat.shape), f32(1, columns)],
-        cost_estimate=pl.CostEstimate(flops=2**23, bytes_accessed=2**20, transcendentals=0),
-    )(gathered, span_order, raw_heat, raw_surf)
+    cos_row, alb_row, live = find_listed(sun_cos, albedo, keep_list, ship_list, ship_count, span_order)
+    heat, surf = radiate(profiles, cos_row, alb_row, live, w_hidden, optical_weight, solar_weight)
     return heat, surf.reshape(-1)
 
 

time: 87.8 us -> 68 us (0.77)
  waiting for transfers between devices: 21.9 us -> 0 us
  Pallas kernels: 51 us -> 66.5 us
  between operations: 14.7 us -> 1.29 us
    all_gather x1 -> x0, waiting for transfers between devices: 21.9 us -> none  [on_device(): gathered = lax.all_gather(flags, ('face', 'tile'), axis=0, tiled=True)]
    pallas_call x2 -> x1, Pallas kernels: 3.73 us -> 18.6 us  [find_listed(): pl.pallas_call(listed_kernel, in_specs=[vmem] * 6, out_specs=[vmem] * 3,...]
  transfers between devices with their start and end apart: 1 -> 0, of which waited for: 1 -> 0; matrix products, arithmetic and copies ran while one was open for 0% -> 0% of each run, Pallas kernels for 54% -> 0%
where the time goes in v3:
time: 68 us; the launch traced here: 67.8 us
  Pallas kernels  66.5 us (98%)
  between operations  1.29 us (2%)
    pallas_call x1, Pallas kernels, radiate(): pl.pallas_call(radiate_kernel, grid=grid, in_specs=[pl.BlockSpec((C, L *...  47.9 us
    pallas_call x1, Pallas kernels, find_listed(): pl.pallas_call(listed_kernel, in_specs=[vmem] * 6, out_specs=[vmem] * 3,...  18.6 us

profile of v3, /device:TPU:1, one launch (start us, length us, event | category | flops | bytes accessed | tf_op | source)
XLA Modules:
  0.0 67.8 jit_solution(3588419262253713161)
XLA Ops:
  1.3 18.6 %shard_map.113 = (f32[1,1024]{1,0:T(1,128)}, f32[1,1024]{1,0:T(1,128)}, f32[1,1024]{1,0:T(1,128)}) custom-call(bf16[1024]{0:T(1024)(128)(2,1)} %cos_ref.1, bf16[1024]{0:T(1024)(128)(2,1)} %alb_ref.1, s32[1,384]{1,0:T(1,128)} %keep_ref.1, s32[1,128]{1,0:T(1,128)} %ship_ref.1, s32[1,1]{1,0:T(1,128)} %bitcast.4.count_ref, s32[1,1024]{1,0:T(1,128)} %order_ref.1), custom_call_target="tpu_custom_call" | custom-call | flops 8388608 | bytes 131072 | tf_op jit(solution)/shard_map/pallas_call | solution.py:262
  19.9 47.9 %shard_map.114 = (f32[64,1024]{1,0:T(8,128)}, f32[1,1024]{1,0:T(1,128)}) custom-call(bf16[1024,2048]{1,0:T(8,128)(2,1)} %prof_ref.1, f32[1,1024]{1,0:T(1,128)} %get-tuple-element.7.cos_ref, f32[1,1024]{1,0:T(1,128)} %get-tuple-element.8.alb_ref, f32[1,1024]{1,0:T(1,128)} %get-tuple-element.9.live_ref, bf16[32,128]{1,0:T(8,128)(2,1)} %wh_ref.1, ...), custom_call_target="tpu_custom_call" | custom-call | flops 6000000000 | bytes 8388608 | tf_op jit(solution)/shard_map/pallas_call | solution.py:157

commit v4 on v2

v4 whole, which is shorter than its diff:
```python
import functools, math
import jax, jax.numpy as jnp
from jax import lax
from jax.experimental import pallas as pl
from jax.experimental.pallas import tpu as pltpu
from jax.sharding import PartitionSpec as P

L, F, H, G = 64, 32, 128, 112
LOG2E = math.log2(math.e)
U = 4
W = 256
GT = 16
DFIRST = False
RENORM = 8

LO, HI = 16, 8


def here():
    tiles = lax.axis_size("tile")
    me = lax.axis_index("face") * tiles + lax.axis_index("tile")
    return me // LO, me % LO


def place(h, l):
    tiles = lax.axis_size("tile")
    device = h * LO + l
    return (device // tiles, device % tiles)


def one_hot(hit):
    return jnp.where(hit, 1.0, 0.0).astype(jnp.bfloat16)


LANES = (((1,), (1,)), ((), ()))


def greet():
    hi, lo = here()
    barrier = pltpu.get_barrier_semaphore()
    for j in range(1, LO):
        pl.semaphore_signal(barrier, inc=1, device_id=place(hi, (lo + j) % LO), device_id_type=pl.DeviceIdType.MESH)
    for j in range(1, HI):
        pl.semaphore_signal(barrier, inc=1, device_id=place((hi + j) % HI, lo), device_id_type=pl.DeviceIdType.MESH)


def make_flags(keep_ref, ship_ref, count_ref, made, per_peer):
    devices = LO * HI
    total = None
    for ref, live_count in ((keep_ref, keep_ref.shape[1]), (ship_ref, count_ref[...])):
        slots = ref[...]
        n = slots.shape[1]
        row = lax.broadcasted_iota(jnp.int32, (devices, n), 0)
        at = lax.broadcasted_iota(jnp.int32, (devices, n), 1)
        peer = (row % HI) * LO + row // HI
        left = one_hot(slots // per_peer == peer)
        right = one_hot((slots % per_peer == row) & (at < live_count))
        part = lax.dot_general(left, right, LANES, preferred_element_type=jnp.float32)
        total = part if total is None else total + part
    made[...] = total.reshape(LO, HI, 128)


def first_copies(made, first, send, recv):
    hi, lo = here()
    out = []
    for j in range(1, LO):
        to = (lo + j) % LO
        out.append(pltpu.make_async_remote_copy(
            src_ref=made.at[to], dst_ref=first.at[lo], send_sem=send.at[j], recv_sem=recv.at[j],
            device_id=place(hi, to), device_id_type=pl.DeviceIdType.MESH))
    return out


def second_copies(turned, second, send, recv):
    hi, lo = here()
    out = []
    for j in range(1, HI):
        to = (hi + j) % HI
        out.append(pltpu.make_async_remote_copy(
            src_ref=turned.at[to], dst_ref=second.at[hi], send_sem=send.at[j], recv_sem=recv.at[j],
            device_id=place(to, lo), device_id_type=pl.DeviceIdType.MESH))
    return out


def listed_columns(second, order_ref, per_peer):
    columns = order_ref.shape[1]
    devices = LO * HI
    got = second[...].reshape(devices, 128).astype(jnp.bfloat16)
    pick = one_hot(lax.broadcasted_iota(jnp.int32, (per_peer, 128), 0) == lax.broadcasted_iota(jnp.int32, (per_peer, 128), 1))
    flags = lax.dot_general(pick, got, LANES, preferred_element_type=jnp.float32).astype(jnp.bfloat16)
    span = lax.broadcasted_iota(jnp.int32, (devices, columns), 0)
    at = lax.broadcasted_iota(jnp.int32, (devices, columns), 1)
    spread = jnp.dot(flags, one_hot(at // per_peer == span), preferred_element_type=jnp.float32)
    share = lax.broadcasted_iota(jnp.int32, (per_peer, columns), 0)
    at8 = lax.broadcasted_iota(jnp.int32, (per_peer, columns), 1)
    flag = jnp.sum(jnp.where(at8 % per_peer == share, spread, 0.0), axis=0, keepdims=True)
    order = order_ref[...]
    group = lax.broadcasted_iota(jnp.int32, (columns // 128, columns), 0)
    lane = lax.broadcasted_iota(jnp.int32, (128, columns), 0)
    placed = jnp.where(order // 128 == group, flag, 0.0).astype(jnp.bfloat16)
    listed = lax.dot_general(placed, one_hot(order % 128 == lane), LANES, preferred_element_type=jnp.float32)
    return listed


def radiate_kernel(prof_ref, cos_ref, alb_ref, keep_ref, ship_ref, count_ref, order_ref, wh_ref, wo_ref, sw_ref,
                   heat_ref, surf_ref,
                   whb, wob, swb, hid, mass_s, k_s, opt, t_s, s_s, inv_s, n_s, d_s, net_s, cos_row, alb_row,
                   made, first, turned, second, send1, recv1, send2, recv2):
    C = prof_ref.shape[0]
    step = pl.program_id(0)
    per_peer = order_ref.shape[1] // (LO * HI)
    mine = pl.ds(pl.multiple_of(step * C, C), C)
    @pl.when(step == 0)
    def _():
        greet()
        make_flags(keep_ref, ship_ref, count_ref, made, per_peer)
        cos_row[...] = cos_ref[...].astype(jnp.float32).reshape(cos_row.shape)
        alb_row[...] = alb_ref[...].astype(jnp.float32).reshape(alb_row.shape)
        whb[...] = jnp.zeros_like(whb)
        wt = (wh_ref[...].astype(jnp.float32) * 0.5).T.astype(jnp.bfloat16)
        for j in range(8):
            whb[j*H:(j+1)*H, j*F:(j+1)*F] = wt
        r = lax.broadcasted_iota(jnp.int32, (16, 256), 0)
        c = lax.broadcasted_iota(jnp.int32, (16, 256), 1)
        whb[8*H:8*H+16, :] = jnp.where(c == r * F, 1.0, 0.0).astype(jnp.bfloat16)
        wob[:G] = wo_ref[:G]
        wob[G:2*G] = (wo_ref[G:2*G].astype(jnp.float32) * 0.5).astype(jnp.bfloat16)
        wob[2*G:] = wo_ref[2*G:]
        swb[...] = jnp.broadcast_to(sw_ref[...], (128, G)).T
    cos = cos_row[:, mine]
    alb = alb_row[:, mine]
    scale = (-2.0 * LOG2E / L) / cos
    n_s[...] = jnp.broadcast_to(alb, (G, C))

    def hidden_chunk(ch, _):
        k0 = pl.multiple_of(ch * 256, 256)
        for s in range(C // W):
            cs = slice(s * W, (s + 1) * W)
            x = prof_ref[cs, pl.ds(k0, 256)]
            pre = lax.dot_general(whb[...], x, (((1,), (1,)), ((), ())), preferred_element_type=jnp.float32)
            h = pre[:8*H]
            hid[pl.ds(pl.multiple_of(ch * 8 * H, 8 * H), 8 * H), cs] = (h + h * jnp.tanh(h)).astype(jnp.bfloat16)
            mass = pre[8*H:8*H+8]
            mass_s[pl.ds(pl.multiple_of(ch * 8, 8), 8), cs] = mass
            kk = mass * scale[:, cs]
            for j in range(8):
                k_s[ch * 8 + j, :, cs] = jnp.broadcast_to(kk[j:j+1], (8, W))
        return 0
    lax.fori_loop(0, 8, hidden_chunk, 0)

    def dots(l, p):
        for u in range(U):
            for s in range(C // W):
                cs = slice(s * W, (s + 1) * W)
                lu = jnp.maximum(l - u, 0)
                opt[p, u, :, cs] = jnp.dot(wob[...], hid[pl.ds(pl.multiple_of(lu * H, H), H), cs], preferred_element_type=jnp.float32)

    def elem(l, p):
        for s in range(C // 128):
            cs = slice(s * 128, (s + 1) * 128)
            for g in range(0, G, GT):
                kv = lambda lv: k_s[lv, :, cs] if GT == 8 else jnp.concatenate([k_s[lv, :, cs]] * (GT // 8), axis=0)
                N = n_s[g:g+GT, cs]
                Dn = d_s[g:g+GT, cs]
                for u in range(U):
                    a = opt[p, u, g:g+GT, cs]
                    b = opt[p, u, G+g:G+g+GT, cs]
                    c = opt[p, u, 2*G+g:2*G+g+GT, cs]
                    D = jnp.exp2(kv(l - u) * jnp.exp2(a * LOG2E))
                    E = 1.0 - D
                    h2 = (0.245 + 0.245 * jnp.tanh(b)) * E
                    w = h2 * (0.8 * jnp.tanh(c))
                    r = h2 - w
                    t = D + (h2 + w)
                    Dn = Dn - r * N
                    N = r * Dn + t * (t * N)
                    t_s[l - u, g:g+GT, cs] = t
                    s_s[l - u, g:g+GT, cs] = Dn - N
                n_s[g:g+GT, cs] = N
                d_s[g:g+GT, cs] = Dn

    dots(L - 1, 0)
    def group(i, _):
        l0 = L - 1 - i * RENORM
        d_s[...] = jnp.ones((G, C), jnp.float32)
        def inner(j, _):
            l = l0 - U * j
            for p in (0, 1):
                @pl.when(lax.rem(j, 2) == p)
                def _():
                    if DFIRST:
                        dots(l - U, 1 - p)
                        elem(l, p)
                    else:
                        elem(l, p)
                        dots(l - U, 1 - p)
            return 0
        lax.fori_loop(0, RENORM // U, inner, 0)
        ch = L // RENORM - 1 - i
        for g in range(0, G, 8):
            inv = pltpu.reciprocal(d_s[g:g+8, :], approx=False)
            inv_s[ch, g:g+8, :] = inv
            n_s[g:g+8, :] = n_s[g:g+8, :] * inv
        return 0
    lax.fori_loop(0, 8 * (8 // RENORM), group, 0)

    V = 128
    for sp in range(C // V):
        cs = slice(sp * V, (sp + 1) * V)
        def down_chunk(ch, down):
            w = list(down)
            rows = []
            for j in range(8):
                l = ch * 8 + j
                if j % RENORM == 0:
                    ii = ch if RENORM == 8 else ch * (8 // RENORM) + j // RENORM
                    w = [w[i] * inv_s[ii, 8*i:8*i+8, cs] for i in range(G // 8)]
                acc = None
                for i in range(G // 8):
                    p = w[i] * s_s[l, 8*i:8*i+8, cs]
                    acc = p if acc is None else acc + p
                    w[i] = w[i] * t_s[l, 8*i:8*i+8, cs]
                rows.append(jnp.sum(acc, axis=0, keepdims=True))
            net_s[pl.ds(pl.multiple_of(ch * 8, 8), 8), cs] = jnp.concatenate(rows, axis=0)
            return tuple(w)
        down = lax.fori_loop(0, 8, down_chunk, tuple(swb[g:g+8, :] * cos[:, cs] for g in range(0, G, 8)))
        acc = down[0]
        for g in range(1, G//8):
            acc = acc + down[g]
        surf = jnp.sum(acc, axis=0, keepdims=True)
        surf_ref[:, pl.ds(pl.multiple_of(step * C + sp * V, V), V)] = surf
        net_s[L:L+1, cs] = surf * (1.0 - alb[:, cs])
    heat_ref[:, mine] = L * (net_s[0:L, :] - net_s[1:L+1, :]) / mass_s[...]

    @pl.when(step == 0)
    def _():
        pl.semaphore_wait(pltpu.get_barrier_semaphore(), LO + HI - 2)
        for copy in first_copies(made, first, send1, recv1):
            copy.start()

    @pl.when(step == 1)
    def _():
        hi, lo = here()
        first[lo] = made[lo]
        for copy in first_copies(made, first, send1, recv1):
            copy.wait()
        turned[...] = jnp.swapaxes(first[...], 0, 1)
        for copy in second_copies(turned, second, send2, recv2):
            copy.start()

    @pl.when(step == 2)
    def _():
        hi, lo = here()
        second[hi] = turned[hi]
        for copy in second_copies(turned, second, send2, recv2):
            copy.wait()

    @pl.when(step == pl.num_programs(0) - 1)
    def _():
        listed = listed_columns(second, order_ref, per_peer)
        for i in range(order_ref.shape[1] // 128):
            cs = slice(i * 128, (i + 1) * 128)
            live = listed[i : i + 1, :] > 0.5
            heat_ref[:, cs] = jnp.where(live, heat_ref[:, cs], 0.0)
            surf_ref[:, cs] = jnp.where(live, surf_ref[:, cs], 0.0)


def on_device(profiles, sun_cos, albedo, span_order, keep_list, ship_list, ship_count, w_hidden, optical_weight, solar_weight):
    N, C = profiles.shape[0], 256
    full = lambda *s: pl.BlockSpec(s, lambda i: (0,) * len(s))
    vmem = pl.BlockSpec(memory_space=pltpu.VMEM)
    vm = lambda *s: pltpu.VMEM(s, jnp.float32)
    vb = lambda *s: pltpu.VMEM(s, jnp.bfloat16)
    dma = pltpu.SemaphoreType.DMA
    heat, surf = pl.pallas_call(
        radiate_kernel,
        grid=(N // C,),
        in_specs=[pl.BlockSpec((C, L*F), lambda i: (i, 0)), vmem, vmem, vmem, vmem, vmem, vmem,
                  full(F, H), full(3*G, H), full(1, G)],
        out_specs=[full(L, N), full(1, N)],
        out_shape=[jax.ShapeDtypeStruct((L, N), jnp.float32), jax.ShapeDtypeStruct((1, N), jnp.float32)],
        scratch_shapes=[vb(8*H+16, 256), vb(3*G, H), vm(G, 128), vb(L*H, C), vm(L, C), vm(L, 8, C),
                        vm(2, U, 3*G, C), vm(L, G, C), vm(L, G, C), vm(L // RENORM, G, C), vm(G, C), vm(G, C), vm(L+8, C),
                        vm(1, N), vm(1, N),
                        vm(LO, HI, 128), vm(LO, HI, 128), vm(HI, LO, 128), vm(HI, LO, 128), dma((LO,)), dma((LO,)), dma((HI,)), dma((HI,))],
        compiler_params=pltpu.CompilerParams(vmem_limit_bytes=60*2**20, collective_id=0, has_side_effects=True),
        cost_estimate=pl.CostEstimate(flops=6*10**9, bytes_accessed=2**23, transcendentals=4*10**7),
    )(profiles, sun_cos, albedo, keep_list, ship_list, ship_count.reshape(1, 1), span_order, w_hidden, optical_weight.T, solar_weight.reshape(1, G))
    return heat, surf.reshape(-1)


def solution(mesh):
    both = ("face", "tile")
    rows, flat = P(both, None), P(both)
    placed = (rows, flat, flat, rows, rows, rows, flat, P(), P(), P())
    return jax.shard_map(on_device, mesh=mesh, in_specs=placed, out_specs=(P(None, both), flat), check_vma=False)
```

time: 87.8 us -> 53 us (0.60)
  waiting for transfers between devices: 21.9 us -> 0 us
  between operations: 14.7 us -> 1.29 us
  local copies, waits for them, and re-layouts: 0 us -> 2.95 us
  Pallas kernels: 51 us -> 48.5 us
    all_gather x1 -> x0, waiting for transfers between devices: 21.9 us -> none  [on_device(): gathered = lax.all_gather(flags, ('face', 'tile'), axis=0, tiled=True)]
    unnamed x0 -> x2, local copies, waits for them, and re-layouts: none -> 2.95 us
    pallas_call x3 -> x1, Pallas kernels: 51 us -> 48.5 us  [on_device(): pl.pallas_call(radiate_kernel, grid=(N // C,), in_specs=[pl.BlockSpec((C,...]
  transfers between devices with their start and end apart: 1 -> 0, of which waited for: 1 -> 0; matrix products, arithmetic and copies ran while one was open for 0% -> 0% of each run, Pallas kernels for 54% -> 0%
where the time goes in v4:
time: 53 us; the launch traced here: 52.8 us
  Pallas kernels  48.5 us (92%)
  local copies, waits for them, and re-layouts  2.95 us (6%)
  between operations  1.29 us (2%)
    pallas_call x1, Pallas kernels, on_device(): pl.pallas_call(radiate_kernel, grid=(N // C,), in_specs=[pl.BlockSpec((C,...  48.5 us
    unnamed x2, local copies, waits for them, and re-layouts  2.95 us

profile of v4, /device:TPU:1, one launch (start us, length us, event | category | flops | bytes accessed | tf_op | source)
XLA Modules:
  0.0 52.8 jit_solution(8498552277558015007)
XLA Ops:
  1.3 48.5 %shard_map.113 = (f32[64,1024]{1,0:T(8,128)}, f32[1,1024]{1,0:T(1,128)}) custom-call(bf16[1024,2048]{1,0:T(8,128)(2,1)} %prof_ref.1, bf16[1024]{0:T(1024)(128)(2,1)} %cos_ref.1, bf16[1024]{0:T(1024)(128)(2,1)} %alb_ref.1, s32[1,384]{1,0:T(1,128)} %keep_ref.1, s32[1,128]{1,0:T(1,128)} %ship_ref.1, s32[1,1]{1,0:T(1,128)} %bitcast.4.count_ref, ...), custom_call_target="tpu_custom_call" | custom-call | flops 6000000000 | bytes 8388608 | tf_op jit(solution)/shard_map/pallas_call | solution.py:275
  49.8 1.7 %copy.15 = f32[64,1024]{1,0:T(8,128)} copy(f32[64,1024]{1,0:T(8,128)} %get-tuple-element.8) | data formatting | bytes 524288
  51.5 1.3 %copy.16 = f32[1024]{0:T(1024)} copy(f32[1024]{0:T(1024)} %bitcast.5) | data formatting | bytes 8192

commit v5 on v4

v5 whole, which is shorter than its diff:
```python
import functools, math
import jax, jax.numpy as jnp
from jax import lax
from jax.experimental import pallas as pl
from jax.experimental.pallas import tpu as pltpu
from jax.sharding import PartitionSpec as P

L, F, H, G = 64, 32, 128, 112
LOG2E = math.log2(math.e)
U = 4
W = 256
GT = 16
DFIRST = False
RENORM = 8

LO, HI = 16, 8


def here():
    tiles = lax.axis_size("tile")
    me = lax.axis_index("face") * tiles + lax.axis_index("tile")
    return me // LO, me % LO


def place(h, l):
    tiles = lax.axis_size("tile")
    device = h * LO + l
    return (device // tiles, device % tiles)


def one_hot(hit):
    return jnp.where(hit, 1.0, 0.0).astype(jnp.bfloat16)


LANES = (((1,), (1,)), ((), ()))


def greet():
    hi, lo = here()
    barrier = pltpu.get_barrier_semaphore()
    for j in range(1, LO):
        pl.semaphore_signal(barrier, inc=1, device_id=place(hi, (lo + j) % LO), device_id_type=pl.DeviceIdType.MESH)
    for j in range(1, HI):
        pl.semaphore_signal(barrier, inc=1, device_id=place((hi + j) % HI, lo), device_id_type=pl.DeviceIdType.MESH)


def make_flags(keep_ref, ship_ref, count_ref, made, per_peer):
    devices = LO * HI
    total = None
    for ref, live_count in ((keep_ref, keep_ref.shape[1]), (ship_ref, count_ref[...])):
        slots = ref[...]
        n = slots.shape[1]
        row = lax.broadcasted_iota(jnp.int32, (devices, n), 0)
        at = lax.broadcasted_iota(jnp.int32, (devices, n), 1)
        peer = (row % HI) * LO + row // HI
        left = one_hot(slots // per_peer == peer)
        right = one_hot((slots % per_peer == row) & (at < live_count))
        part = lax.dot_general(left, right, LANES, preferred_element_type=jnp.float32)
        total = part if total is None else total + part
    made[...] = total.reshape(LO, HI, 128)


def first_copies(made, first, send, recv):
    hi, lo = here()
    out = []
    for j in range(1, LO):
        to = (lo + j) % LO
        out.append(pltpu.make_async_remote_copy(
            src_ref=made.at[to], dst_ref=first.at[lo], send_sem=send.at[j], recv_sem=recv.at[j],
            device_id=place(hi, to), device_id_type=pl.DeviceIdType.MESH))
    return out


def second_copies(turned, second, send, recv):
    hi, lo = here()
    out = []
    for j in range(1, HI):
        to = (hi + j) % HI
        out.append(pltpu.make_async_remote_copy(
            src_ref=turned.at[to], dst_ref=second.at[hi], send_sem=send.at[j], recv_sem=recv.at[j],
            device_id=place(to, lo), device_id_type=pl.DeviceIdType.MESH))
    return out


def listed_columns(second, order_ref, per_peer):
    columns = order_ref.shape[1]
    devices = LO * HI
    got = second[...].reshape(devices, 128).astype(jnp.bfloat16)
    pick = one_hot(lax.broadcasted_iota(jnp.int32, (per_peer, 128), 0) == lax.broadcasted_iota(jnp.int32, (per_peer, 128), 1))
    flags = lax.dot_general(pick, got, LANES, preferred_element_type=jnp.float32).astype(jnp.bfloat16)
    span = lax.broadcasted_iota(jnp.int32, (devices, columns), 0)
    at = lax.broadcasted_iota(jnp.int32, (devices, columns), 1)
    spread = jnp.dot(flags, one_hot(at // per_peer == span), preferred_element_type=jnp.float32)
    share = lax.broadcasted_iota(jnp.int32, (per_peer, columns), 0)
    at8 = lax.broadcasted_iota(jnp.int32, (per_peer, columns), 1)
    flag = jnp.sum(jnp.where(at8 % per_peer == share, spread, 0.0), axis=0, keepdims=True)
    order = order_ref[...]
    group = lax.broadcasted_iota(jnp.int32, (columns // 128, columns), 0)
    lane = lax.broadcasted_iota(jnp.int32, (128, columns), 0)
    placed = jnp.where(order // 128 == group, flag, 0.0).astype(jnp.bfloat16)
    listed = lax.dot_general(placed, one_hot(order % 128 == lane), LANES, preferred_element_type=jnp.float32)
    return listed


def radiate_kernel(prof_ref, cos_ref, alb_ref, keep_ref, ship_ref, count_ref, order_ref, wh_ref, wo_ref, sw_ref,
                   heat_ref, surf_ref, live_ref,
                   whb, wob, swb, hid, mass_s, k_s, opt, t_s, s_s, inv_s, n_s, d_s, net_s, cos_row, alb_row,
                   made, first, turned, second, send1, recv1, send2, recv2):
    halves, C = prof_ref.shape[0] // W, W
    step = pl.program_id(0)
    per_peer = order_ref.shape[1] // (LO * HI)
    @pl.when(step == 0)
    def _():
        greet()
        make_flags(keep_ref, ship_ref, count_ref, made, per_peer)
        cos_row[...] = cos_ref[...].astype(jnp.float32).reshape(cos_row.shape)
        alb_row[...] = alb_ref[...].astype(jnp.float32).reshape(alb_row.shape)
        whb[...] = jnp.zeros_like(whb)
        wt = (wh_ref[...].astype(jnp.float32) * 0.5).T.astype(jnp.bfloat16)
        for j in range(8):
            whb[j*H:(j+1)*H, j*F:(j+1)*F] = wt
        r = lax.broadcasted_iota(jnp.int32, (16, 256), 0)
        c = lax.broadcasted_iota(jnp.int32, (16, 256), 1)
        whb[8*H:8*H+16, :] = jnp.where(c == r * F, 1.0, 0.0).astype(jnp.bfloat16)
        wob[:G] = wo_ref[:G]
        wob[G:2*G] = (wo_ref[G:2*G].astype(jnp.float32) * 0.5).astype(jnp.bfloat16)
        wob[2*G:] = wo_ref[2*G:]
        swb[...] = jnp.broadcast_to(sw_ref[...], (128, G)).T
    def hidden_chunk(ch, _):
        k0 = pl.multiple_of(ch * 256, 256)
        for s in range(halves):
            x = prof_ref[s * W : (s + 1) * W, pl.ds(k0, 256)]
            pre = lax.dot_general(whb[...], x, (((1,), (1,)), ((), ())), preferred_element_type=jnp.float32)
            h = pre[:8*H]
            hid[s, pl.ds(pl.multiple_of(ch * 8 * H, 8 * H), 8 * H), :] = (h + h * jnp.tanh(h)).astype(jnp.bfloat16)
            mass = pre[8*H:8*H+8]
            mass_s[s, pl.ds(pl.multiple_of(ch * 8, 8), 8), :] = mass
            scale = (-2.0 * LOG2E / L) / cos_row[:, pl.ds(pl.multiple_of((step * halves + s) * W, W), W)]
            kk = mass * scale
            for j in range(8):
                k_s[s, ch * 8 + j] = jnp.broadcast_to(kk[j:j+1], (8, W))
        return 0
    lax.fori_loop(0, 8, hidden_chunk, 0)

    def one_half(half, _):
        q = step * halves + half
        mine = pl.ds(pl.multiple_of(q * C, C), C)
        cos = cos_row[:, mine]
        alb = alb_row[:, mine]
        n_s[...] = jnp.broadcast_to(alb, (G, C))

        def dots(l, p):
            for u in range(U):
                lu = jnp.maximum(l - u, 0)
                opt[p, u] = jnp.dot(wob[...], hid[half, pl.ds(pl.multiple_of(lu * H, H), H), :], preferred_element_type=jnp.float32)

        def elem(l, p):
            for s in range(C // 128):
                cs = slice(s * 128, (s + 1) * 128)
                for g in range(0, G, GT):
                    kv = lambda lv: k_s[half, lv, :, cs] if GT == 8 else jnp.concatenate([k_s[half, lv, :, cs]] * (GT // 8), axis=0)
                    N = n_s[g:g+GT, cs]
                    Dn = d_s[g:g+GT, cs]
                    for u in range(U):
                        a = opt[p, u, g:g+GT, cs]
                        b = opt[p, u, G+g:G+g+GT, cs]
                        c = opt[p, u, 2*G+g:2*G+g+GT, cs]
                        D = jnp.exp2(kv(l - u) * jnp.exp2(a * LOG2E))
                        E = 1.0 - D
                        h2 = (0.245 + 0.245 * jnp.tanh(b)) * E
                        w = h2 * (0.8 * jnp.tanh(c))
                        r = h2 - w
                        t = D + (h2 + w)
                        Dn = Dn - r * N
                        N = r * Dn + t * (t * N)
                        t_s[l - u, g:g+GT, cs] = t
                        s_s[l - u, g:g+GT, cs] = Dn - N
                    n_s[g:g+GT, cs] = N
                    d_s[g:g+GT, cs] = Dn

        dots(L - 1, 0)
        def group(i, _):
            l0 = L - 1 - i * RENORM
            d_s[...] = jnp.ones((G, C), jnp.float32)
            def inner(j, _):
                l = l0 - U * j
                for p in (0, 1):
                    @pl.when(lax.rem(j, 2) == p)
                    def _():
                        if DFIRST:
                            dots(l - U, 1 - p)
                            elem(l, p)
                        else:
                            elem(l, p)
                            dots(l - U, 1 - p)
                return 0
            lax.fori_loop(0, RENORM // U, inner, 0)
            ch = L // RENORM - 1 - i
            for g in range(0, G, 8):
                inv = pltpu.reciprocal(d_s[g:g+8, :], approx=False)
                inv_s[ch, g:g+8, :] = inv
                n_s[g:g+8, :] = n_s[g:g+8, :] * inv
            return 0
        lax.fori_loop(0, 8 * (8 // RENORM), group, 0)

        V = 128
        for sp in range(C // V):
            cs = slice(sp * V, (sp + 1) * V)
            def down_chunk(ch, down):
                w = list(down)
                rows = []
                for j in range(8):
                    l = ch * 8 + j
                    if j % RENORM == 0:
                        ii = ch if RENORM == 8 else ch * (8 // RENORM) + j // RENORM
                        w = [w[i] * inv_s[ii, 8*i:8*i+8, cs] for i in range(G // 8)]
                    acc = None
                    for i in range(G // 8):
                        p = w[i] * s_s[l, 8*i:8*i+8, cs]
                        acc = p if acc is None else acc + p
                        w[i] = w[i] * t_s[l, 8*i:8*i+8, cs]
                    rows.append(jnp.sum(acc, axis=0, keepdims=True))
                net_s[pl.ds(pl.multiple_of(ch * 8, 8), 8), cs] = jnp.concatenate(rows, axis=0)
                return tuple(w)
            down = lax.fori_loop(0, 8, down_chunk, tuple(swb[g:g+8, :] * cos[:, cs] for g in range(0, G, 8)))
            acc = down[0]
            for g in range(1, G//8):
                acc = acc + down[g]
            surf = jnp.sum(acc, axis=0, keepdims=True)
            surf_ref[:, pl.ds(pl.multiple_of(q * C + sp * V, V), V)] = surf
            net_s[L:L+1, cs] = surf * (1.0 - alb[:, cs])
        heat_ref[:, mine] = L * (net_s[0:L, :] - net_s[1:L+1, :]) / mass_s[half]

        @pl.when(q == 0)
        def _():
            pl.semaphore_wait(pltpu.get_barrier_semaphore(), LO + HI - 2)
            for copy in first_copies(made, first, send1, recv1):
                copy.start()

        @pl.when(q == 1)
        def _():
            hi, lo = here()
            first[lo] = made[lo]
            for copy in first_copies(made, first, send1, recv1):
                copy.wait()
            turned[...] = jnp.swapaxes(first[...], 0, 1)
            for copy in second_copies(turned, second, send2, recv2):
                copy.start()

        @pl.when(q == 2)
        def _():
            hi, lo = here()
            second[hi] = turned[hi]
            for copy in second_copies(turned, second, send2, recv2):
                copy.wait()
        return 0

    lax.fori_loop(0, halves, one_half, 0)

    @pl.when(step == pl.num_programs(0) - 1)
    def _():
        listed = listed_columns(second, order_ref, per_peer)
        for i in range(order_ref.shape[1] // 128):
            live_ref[:, i * 128 : (i + 1) * 128] = listed[i : i + 1, :]


def zero_kernel(raw_heat_ref, raw_surf_ref, live_ref, heat_ref, surf_ref):
    live = live_ref[...] > 0.5
    heat_ref[...] = jnp.where(live, raw_heat_ref[...], 0.0)
    surf_ref[...] = jnp.where(live, raw_surf_ref[...], 0.0)


def on_device(profiles, sun_cos, albedo, span_order, keep_list, ship_list, ship_count, w_hidden, optical_weight, solar_weight):
    N, C = profiles.shape[0], 2 * W
    full = lambda *s: pl.BlockSpec(s, lambda i: (0,) * len(s))
    vmem = pl.BlockSpec(memory_space=pltpu.VMEM)
    vm = lambda *s: pltpu.VMEM(s, jnp.float32)
    vb = lambda *s: pltpu.VMEM(s, jnp.bfloat16)
    dma = pltpu.SemaphoreType.DMA
    raw_heat, raw_surf, live = pl.pallas_call(
        radiate_kernel,
        grid=(N // C,),
        in_specs=[pl.BlockSpec((C, L*F), lambda i: (i, 0)), vmem, vmem, vmem, vmem, vmem, vmem,
                  full(F, H), full(3*G, H), full(1, G)],
        out_specs=[full(L, N), full(1, N), full(1, N)],
        out_shape=[jax.ShapeDtypeStruct((n, N), jnp.float32) for n in (L, 1, 1)],
        scratch_shapes=[vb(8*H+16, 256), vb(3*G, H), vm(G, 128), vb(C // W, L*H, W), vm(C // W, L, W), vm(C // W, L, 8, W),
                        vm(2, U, 3*G, W), vm(L, G, W), vm(L, G, W), vm(L // RENORM, G, W), vm(G, W), vm(G, W), vm(L+8, W),
                        vm(1, N), vm(1, N),
                        vm(LO, HI, 128), vm(LO, HI, 128), vm(HI, LO, 128), vm(HI, LO, 128), dma((LO,)), dma((LO,)), dma((HI,)), dma((HI,))],
        compiler_params=pltpu.CompilerParams(vmem_limit_bytes=60*2**20, collective_id=0, has_side_effects=True),
        cost_estimate=pl.CostEstimate(flops=6*10**9, bytes_accessed=2**23, transcendentals=4*10**7),
    )(profiles, sun_cos, albedo, keep_list, ship_list, ship_count.reshape(1, 1), span_order, w_hidden, optical_weight.T, solar_weight.reshape(1, G))
    heat, surf = pl.pallas_call(
        zero_kernel,
        out_shape=[jax.ShapeDtypeStruct((n, N), jnp.float32) for n in (L, 1)],
        cost_estimate=pl.CostEstimate(flops=2**17, bytes_accessed=2**19, transcendentals=0),
    )(raw_heat, raw_surf, live)
    return heat, surf.reshape(-1)


def solution(mesh):
    both = ("face", "tile")
    rows, flat = P(both, None), P(both)
    placed = (rows, flat, flat, rows, rows, rows, flat, P(), P(), P())
    return jax.shard_map(on_device, mesh=mesh, in_specs=placed, out_specs=(P(None, both), flat), check_vma=False)
```

time: 53 us -> 48.4 us (0.913)
  local copies, waits for them, and re-layouts: 2.95 us -> 0 us
  Pallas kernels: 48.5 us -> 47 us
    pallas_call x1, Pallas kernels: 48.5 us -> 45.3 us  [on_device(): pl.pallas_call(radiate_kernel, grid=(N // C,), in_specs=[pl.BlockSpec((C,...]
    unnamed x2 -> x0, local copies, waits for them, and re-layouts: 2.95 us -> none
    pallas_call x0 -> x1, Pallas kernels: none -> 1.68 us  [on_device(): pl.pallas_call(zero_kernel, out_shape=[jax.ShapeDtypeStruct((n, N), jnp.f...]
where the time goes in v5:
time: 48.4 us; the launch traced here: 48.3 us
  Pallas kernels  47 us (97%)
  between operations  1.29 us (3%)
    pallas_call x1, Pallas kernels, on_device(): pl.pallas_call(radiate_kernel, grid=(N // C,), in_specs=[pl.BlockSpec((C,...  45.3 us
    pallas_call x1, Pallas kernels, on_device(): pl.pallas_call(zero_kernel, out_shape=[jax.ShapeDtypeStruct((n, N), jnp.f...  1.68 us

profile of v5, /device:TPU:1, one launch (start us, length us, event | category | flops | bytes accessed | tf_op | source)
XLA Modules:
  0.0 48.3 jit_solution(5201648359222173411)
XLA Ops:
  1.3 45.3 %shard_map.113 = (f32[64,1024]{1,0:T(8,128)}, f32[1,1024]{1,0:T(1,128)}, f32[1,1024]{1,0:T(1,128)}) custom-call(bf16[1024,2048]{1,0:T(8,128)(2,1)} %prof_ref.1, bf16[1024]{0:T(1024)(128)(2,1)} %cos_ref.1, bf16[1024]{0:T(1024)(128)(2,1)} %alb_ref.1, s32[1,384]{1,0:T(1,128)} %keep_ref.1, s32[1,128]{1,0:T(1,128)} %ship_ref.1, s32[1,1]{1,0:T(1,128)} %bitcast.4.count_ref, ...), custom_call_target="tpu_custom_call" | custom-call | flops 6000000000 | bytes 8388608 | tf_op jit(solution)/shard_map/pallas_call | solution.py:280
  46.6 1.7 %shard_map.114 = (f32[64,1024]{1,0:T(8,128)}, f32[1,1024]{1,0:T(1,128)}) custom-call(f32[64,1024]{1,0:T(8,128)} %get-tuple-element.7.raw_heat_ref, f32[1,1024]{1,0:T(1,128)} %get-tuple-element.8.raw_surf_ref, f32[1,1024]{1,0:T(1,128)} %get-tuple-element.9.live_ref), custom_call_target="tpu_custom_call" | custom-call | flops 131072 | bytes 524288 | tf_op jit(solution)/shard_map/pallas_call | solution.py:294
